TPU v7x, 512 devices: a whole 4x4x16 slice. The times are simulated.
512 devices in a mesh: seq: 256 (over x, z, y_lo, core), rep: 2 (over y_hi).
Axes of the slice: x: 4, y: 4 (y_hi: 2, y_lo: 2; y = y_hi * 2 + y_lo), z: 16, core: 2. Of those that a mesh axis runs over, the one named last changes fastest.
Arguments:
- acts: bfloat16 [131072, 6144], P(('seq', 'rep')), may hold values from -24 to 24
- grad_logits: bfloat16 [131072, 128], P(('seq', 'rep')), may hold values from -0.017944336 to 0.017944336
- master: float32 [6144, 128], P('seq'), may hold values from -0.078125 to 0.078125
- moment_one: float32 [6144, 128], P('seq'), may hold values from -3 to 3
- moment_two: float32 [6144, 128], P('seq'), may hold values from 0.05 to 2
- step_count: int32 [1], replicated, may hold values from 1 to 40
Outputs:
- master_new: float32 [6144, 128], P('seq')
- moment_one_new: float32 [6144, 128], P('seq')
- moment_two_new: float32 [6144, 128], P('seq')
- logits_new: bfloat16 [131072, 128], P(('seq', 'rep'))
All inputs are finite; a program needn't handle non-finite values.
Results may differ from a plain program's by a relative error of at most 0.0024.
The roundings to bfloat16 on the way count: a program that leaves them out, or rounds other values in their place, can miss the bound.
Values may be sent and summed in bfloat16 or wider, within the bound.
A program may use at most 64 MiB of HBM per device.

v0:
```python
import jax
import jax.numpy as jnp
from jax import lax
from jax.sharding import PartitionSpec as P


def per_device(acts, grad_logits, master, moment_one, moment_two, step_count):
    columns = acts
    product = lax.dot_general(
        columns, grad_logits, (((0,), (0,)), ((), ())), preferred_element_type=jnp.float32
    )
    rounded = lax.optimization_barrier(product.astype(jnp.bfloat16))
    row_grad = lax.psum_scatter(rounded.astype(jnp.float32), "seq", scatter_dimension=0, tiled=True)
    grad = lax.psum(row_grad, "rep")
    count = step_count[0].astype(jnp.float32)
    beta_one = 0.9
    beta_two = 0.95
    first = beta_one * moment_one + (1.0 - beta_one) * grad
    second = beta_two * moment_two + (1.0 - beta_two) * grad * grad
    first_hat = first / (1.0 - jnp.power(beta_one, count))
    second_hat = second / (1.0 - jnp.power(beta_two, count))
    updated = master - 0.01 * (first_hat / (jnp.sqrt(second_hat) + 1e-08) + 0.1 * master)
    weight_new = updated.astype(jnp.bfloat16)
    columns = acts
    logits = jnp.dot(
        columns,
        lax.all_gather(weight_new, "seq", axis=0, tiled=True),
        preferred_element_type=jnp.float32,
    )
    return (updated, first, second, logits.astype(jnp.bfloat16))


def solution(mesh):
    in_specs = (
        P(("seq", "rep"), None),
        P(("seq", "rep"), None),
        P("seq", None),
        P("seq", None),
        P("seq", None),
        P(),
    )
    out_specs = (P("seq", None), P("seq", None), P("seq", None), P(("seq", "rep"), None))
    return jax.shard_map(
        per_device, mesh=mesh, in_specs=in_specs, out_specs=out_specs, check_vma=False
    )
```

profile of v0, /device:TPU:1, one launch (start us, length us, event | category | flops | bytes accessed | tf_op | source)
XLA Modules:
  0.0 1563.5 jit_solution(4956616690435630787)
XLA Ops:
  7.2 0.0 copy-start
  7.2 0.0 reduce-scatter.5.cloned.1.call-start
  7.2 1.8 copy-done
  9.1 1.9 convolution_convert_fusion
  10.9 0.0 copy-start.1
  11.0 0.0 copy-start.2
  11.0 0.0 copy-start.3
  11.0 1.9 convert_element_type.20
  12.8 0.0 reduce-scatter.5.cloned.1.call-update
  12.9 0.0 all-gather.2.cloned.1.call-start
  13.6 1125.2 %reduce-scatter.5.cloned.1.call-done = f32[24,128]{1,0:T(8,128)} async-done(((f32[6144,128]{1,0:T(8,128)}), f32[24,128]{1,0:T(8,128)}) %reduce-scatter.5.cloned.1.call-update) | async-done | bytes 12304
  1138.9 9.5 psum.7
  1148.4 0.0 copy-done.1
  1148.4 0.0 copy-done.2
  1148.4 0.0 copy-done.3
  1148.4 0.6 fusion.2
  1149.0 0.0 all-gather.2.cloned.1.call-update
  1149.1 404.3 %all-gather.2.cloned.1.call-done = bf16[6144,128]{1,0:T(8,128)(2,1)} async-done(((bf16[24,128]{1,0:T(8,128)(2,1)}), bf16[6144,128]{1,0:T(8,128)(2,1)}) %all-gather.2.cloned.1.call-update) | async-done | bytes 1572880 | tf_op jit(solution)/shard_map/all_gather | solution.py:27
  1553.4 2.6 fusion
  1556.0 0.7 copy.11
Async XLA Ops:
  7.2 1.9 copy-start
  7.2 1131.7 %reduce-scatter.5.cloned.1.call-start = ((), (), s32[]{:S(2)}) async-start(), calls=%async_computation.2 | async-start | bytes 3158016
  10.9 1137.4 %copy-start.1 = (f32[24,128]{1,0:T(8,128)S(1)}, f32[24,128]{1,0:T(8,128)}, u32[]{:S(2)}) copy-start(f32[24,128]{1,0:T(8,128)} %param.8) | copy-start | bytes 36868
  11.0 1137.4 %copy-start.2 = (f32[24,128]{1,0:T(8,128)S(1)}, f32[24,128]{1,0:T(8,128)}, u32[]{:S(2)}) copy-start(f32[24,128]{1,0:T(8,128)} %param.10) | copy-start | bytes 36868
  11.0 1137.4 %copy-start.3 = (f32[24,128]{1,0:T(8,128)S(1)}, f32[24,128]{1,0:T(8,128)}, u32[]{:S(2)}) copy-start(f32[24,128]{1,0:T(8,128)} %param.9) | copy-start | bytes 36868
  12.9 1540.5 %all-gather.2.cloned.1.call-start = ((), (), s32[]{:S(2)}) async-start(), calls=%async_computation.1 | async-start | bytes 1579008 | tf_op jit(solution)/shard_map/all_gather | solution.py:27
Sparse Core Ops, SparseCore 0:
  13.0 1125.8 reduce-scatter.4
  1149.2 404.1 all-gather.1
where the time goes:
time: 1570 us; the launch traced here: 1560 us
  waiting for transfers between devices  1530 us (97%)
    unnamed x3, waiting for transfers between devices  1130 us
    all_gather x1, waiting for transfers between devices, per_device(): lax.all_gather(weight_new, 'seq', axis=0, tiled=True)  404 us
  transfers between devices with their start and end apart: 2, of which 2 were waited for; matrix products, arithmetic and copies ran while one was open for 0% of the time, Pallas kernels for 0%

commit v1 on v0

v1 whole, which is shorter than its diff:
```python
import math

import jax
import jax.numpy as jnp
from jax import lax
from jax.experimental import pallas as pl
from jax.experimental.pallas import tpu as pltpu
from jax.sharding import PartitionSpec as P

D = 6144
E = 128
TOK = 256
OWN = 24
UNIT = 48
BLK = 384
F32 = jnp.float32
BF16 = jnp.bfloat16
PAIRS = ((2, 0), (2, 1), (1, 0), (3, 0), (1, 1), (3, 1), (0, 1))
NEAR = ((0, 1), (1, 0), (3, 0), (1, 1), (3, 1), (2, 0), (2, 1))


def adam(grad, master, one, two, count):
    ones = jnp.ones((1, E), F32)
    first = 0.9 * one + (1.0 - 0.9) * grad
    second = 0.95 * two + (1.0 - 0.95) * grad * grad
    first_hat = first / (1.0 - jnp.exp(count * math.log(0.9) * ones))
    second_hat = second / (1.0 - jnp.exp(count * math.log(0.95) * ones))
    updated = master - 0.01 * (first_hat / (jnp.sqrt(second_hat) + 1e-08) + 0.1 * master)
    return updated, first, second


def kernel(
    step_ref, acts_hbm, glog_ref, master_ref, one_ref, two_ref,
    master_out, one_out, two_out, logits_out,
    acts, part, recv_a, acc, recv_b, unit, recv_c, own48, state, state48, grad_own, wnew,
    load_sem, st_sem, sa, ra, sb, rb, sc, rc, sd, rd, sz, rz, s1, r1, s2, r2, s3, r3,
):
    seq = lax.axis_index("seq")
    rep = lax.axis_index("rep")
    core = lax.rem(seq, 2)
    y = rep * 2 + lax.rem(seq // 2, 2)
    z = lax.rem(seq // 4, 16)
    x = seq // 64
    main = (x, y)
    cross = (y, x)

    def dev(px, py, pz, pc):
        return {"seq": ((px * 16 + pz) * 2 + lax.rem(py, 2)) * 2 + pc, "rep": py // 2}

    def at(h, dmain, dcross, dcore):
        dx, dy = (dmain, dcross) if h == 0 else (dcross, dmain)
        return dev(lax.rem(x + dx, 4), lax.rem(y + dy, 4), z, lax.rem(core + dcore, 2))

    def along_z(dz):
        return dev(x, y, lax.rem(z + dz, 16), core)

    barrier = pltpu.get_barrier_semaphore()
    loads = []
    for k in range(4):
        cols = pl.ds(k * 1536, 1536)
        load = pltpu.make_async_copy(acts_hbm.at[:, cols], acts.at[:, cols], load_sem.at[k])
        load.start()
        loads.append(load)
    for h in range(2):
        for d, e in PAIRS:
            if h == 1 and d == 0:
                continue
            pl.semaphore_signal(barrier, inc=1, device_id=at(h, d, 0, e), device_id_type=pl.DeviceIdType.MESH)
    for dz in range(1, 16):
        pl.semaphore_signal(barrier, inc=1, device_id=along_z(dz), device_id_type=pl.DeviceIdType.MESH)

    state[0] = master_ref[...]
    state[1] = one_ref[...]
    state[2] = two_ref[...]
    half = pl.ds(pl.multiple_of(core * OWN, 8), OWN)
    state48[:, half, :] = state[...]

    glog = glog_ref[...]
    for k in range(4):
        loads[k].wait()
        for zg in range(4):
            cols = pl.ds(k * 1536 + zg * BLK, BLK)
            product = lax.dot_general(
                acts[:, cols], glog, (((0,), (0,)), ((), ())), preferred_element_type=F32
            ).astype(BF16)
            for zr in range(4):
                for ylo in range(2):
                    piece = product[(zr * 2 + ylo) * UNIT:(zr * 2 + ylo + 1) * UNIT]
                    py = (zr // 2) * 2 + ylo
                    pc = zr % 2
                    if zg < 2:
                        part[0, k * 2 + pc, py * 96 + zg * UNIT:py * 96 + zg * UNIT + UNIT] = piece
                    else:
                        lo = k * 96 + (zg - 2) * UNIT
                        part[1, py * 2 + pc, lo:lo + UNIT] = piece

    pl.semaphore_wait(barrier, 28)

    def remote(src, dst, send, recv, device):
        return pltpu.make_async_remote_copy(
            src_ref=src, dst_ref=dst, send_sem=send, recv_sem=recv,
            device_id=device, device_id_type=pl.DeviceIdType.MESH,
        )

    sent = []
    copy_a = {}
    for d, e in PAIRS:
        for h in range(2):
            place = lax.rem(main[h] + d, 4) * 2 + lax.rem(core + e, 2)
            copy = remote(
                part.at[h, place], recv_a.at[h, d * 2 + e], sa.at[h, d * 2 + e], ra.at[h, d * 2 + e],
                at(h, d, 0, e),
            )
            copy.start()
            copy_a[h, d, e] = copy
            sent.append(copy)
    state_copy = remote(state, state48.at[:, half, :], st_sem.at[0], st_sem.at[1], at(0, 0, 0, 1))
    state_copy.start()
    sent.append(state_copy)

    copy_b = {}
    for h in range(2):
        mine = main[h] * 2 + core
        for d, e in NEAR:
            copy_a[h, d, e].wait_recv()
        for d in (2, 1, 3, 0):
            to = lax.rem(cross[h] + d, 4)
            rows = pl.ds(pl.multiple_of(to * 96, 16), 96)
            total = part[h, mine, rows].astype(F32)
            for p, e in NEAR:
                total = total + recv_a[h, p * 2 + e, rows].astype(F32)
            acc[h, d] = total
            if d:
                copy = remote(acc.at[h, d], recv_b.at[h, d], sb.at[h, d], rb.at[h, d], at(h, 0, d, 0))
                copy.start()
                copy_b[h, d] = copy
                sent.append(copy)

    mod = rep * 2 + core
    primary = lax.rem(z, 4) == mod
    copy_c = []
    for h in range(2):
        for d in (1, 3, 2):
            copy_b[h, d].wait_recv()
        total = ((acc[h, 0] + recv_b[h, 1]) + recv_b[h, 3]) + recv_b[h, 2]
        for k in range(2):
            zg = h * 2 + k
            unit[zg] = total[k * UNIT:(k + 1) * UNIT]
            to = zg * 4 + mod
            dz = lax.rem(to + 16 - z, 16)
            copy = remote(unit.at[zg], recv_c.at[dz], sc.at[zg], rc.at[dz], dev(x, y, to, core))
            copy_c.append((copy, dz))

            @pl.when(dz != 0)
            def _():
                copy.start()

            @pl.when(dz == 0)
            def _():
                own48[...] = unit[zg]

    count = step_ref[0].astype(F32)
    state_copy.wait_recv()
    other = pl.ds(pl.multiple_of((1 - core) * OWN, 8), OWN)

    def place(h, k):
        which = x * (1 - h) + y * h
        inner = y * (1 - h) + x * h
        return wnew.at[h, which * 2 + core, pl.ds(pl.multiple_of(inner * 96 + k * UNIT, 16), UNIT)]

    zg_me = z // 4
    spot = place(zg_me // 2, lax.rem(zg_me, 2))
    copy_z = [
        remote(spot, spot, sz.at[dz], rz.at[zg_me], along_z(dz)) for dz in range(1, 16)
    ]
    copy_d = [
        remote(own48.at[half], grad_own, sd.at[0], rd.at[0], at(1, 2, 0, 0)),
        remote(own48.at[other], grad_own, sd.at[1], rd.at[0], at(1, 0, 0, 1)),
        remote(own48.at[other], grad_own, sd.at[2], rd.at[0], at(1, 2, 0, 1)),
    ]

    @pl.when(primary)
    def _():
        for dz in range(1, 16):
            remote(recv_c.at[dz], recv_c.at[dz], sc.at[0], rc.at[dz], along_z(dz)).wait_recv()
        total = own48[...]
        for dz in range(1, 16):
            total = total + recv_c[dz]
        updated, _, _ = adam(total, state48[0], state48[1], state48[2], count)
        spot[...] = updated.astype(BF16)
        for dz in (8, 7, 9, 6, 10, 5, 11, 4, 12, 3, 13, 2, 14, 1, 15):
            copy_z[dz - 1].start()
        own48[...] = total
        for copy in copy_d:
            copy.start()
        grad_own[...] = own48[half]

    copy_1 = {}
    for h in range(2):
        for k in range(2):
            zg = h * 2 + k

            @pl.when(z != zg * 4 + mod)
            def _():
                remote(place(h, k), place(h, k), sz.at[0], rz.at[zg], along_z(1)).wait_recv()
        rows = wnew.at[h, main[h] * 2 + core, pl.ds(pl.multiple_of(cross[h] * 96, 16), 96)]
        for d in (2, 1, 3):
            copy = remote(rows, rows, s1.at[h, d], r1.at[h, d], at(h, 0, d, 0))
            copy.start()
            copy_1[h, d] = copy
            sent.append(copy)

    copy_2 = {}
    copy_3 = {}

    def forward(h, d):
        lane = wnew.at[h, lax.rem(main[h] + d, 4) * 2 + core]
        copy = remote(lane, lane, s3.at[h, d], r3.at[h, d], at(h, 0, 0, 1))
        copy.start()
        copy_3[h, d] = copy
        sent.append(copy)

    for h in range(2):
        for d in (1, 3, 2):
            copy_1[h, d].wait_recv()
        block = wnew.at[h, main[h] * 2 + core]
        for d in (2, 1, 3):
            copy = remote(block, block, s2.at[h, d], r2.at[h, d], at(h, d, 0, 0))
            copy.start()
            copy_2[h, d] = copy
            sent.append(copy)
        forward(h, 0)

    @pl.when(jnp.logical_not(primary))
    def _():
        remote(grad_own, grad_own, sd.at[0], rd.at[0], at(1, 2, 0, 0)).wait_recv()

    updated, first, second = adam(grad_own[...], state[0], state[1], state[2], count)
    master_out[...] = updated
    one_out[...] = first
    two_out[...] = second

    for d in (1, 3, 2):
        for h in range(2):
            copy_2[h, d].wait_recv()
            forward(h, 4 - d)
    for d in (0, 1, 3, 2):
        for h in range(2):
            copy_3[h, d].wait_recv()

    total = jnp.zeros((TOK, E), F32)
    for k in range(4):
        for zg in range(4):
            pieces = []
            for zr in range(4):
                for ylo in range(2):
                    py = (zr // 2) * 2 + ylo
                    pc = zr % 2
                    if zg < 2:
                        lo = py * 96 + zg * UNIT
                        pieces.append(wnew[0, k * 2 + pc, lo:lo + UNIT])
                    else:
                        lo = k * 96 + (zg - 2) * UNIT
                        pieces.append(wnew[1, py * 2 + pc, lo:lo + UNIT])
            cols = pl.ds(k * 1536 + zg * BLK, BLK)
            total = total + jnp.dot(
                acts[:, cols], jnp.concatenate(pieces, axis=0), preferred_element_type=F32
            )
    logits_out[...] = total.astype(BF16)

    for copy in sent:
        copy.wait_send()
    for copy, dz in copy_c:
        @pl.when(dz != 0)
        def _():
            copy.wait_send()

    @pl.when(primary)
    def _():
        for copy in copy_z:
            copy.wait_send()
        for copy in copy_d:
            copy.wait_send()


def per_device(acts, grad_logits, master, moment_one, moment_two, step_count):
    vmem = pl.BlockSpec(memory_space=pltpu.VMEM)
    dma = pltpu.SemaphoreType.DMA
    own = jax.ShapeDtypeStruct((OWN, E), F32)
    return pl.pallas_call(
        kernel,
        out_shape=(own, own, own, jax.ShapeDtypeStruct((TOK, E), BF16)),
        in_specs=[
            pl.BlockSpec(memory_space=pltpu.SMEM), pl.BlockSpec(memory_space=pl.ANY), vmem, vmem, vmem, vmem,
        ],
        out_specs=(vmem, vmem, vmem, vmem),
        scratch_shapes=[
            pltpu.VMEM((TOK, D), BF16),
            pltpu.VMEM((2, 8, BLK, E), BF16),
            pltpu.VMEM((2, 8, BLK, E), BF16),
            pltpu.VMEM((2, 4, 96, E), F32),
            pltpu.VMEM((2, 4, 96, E), F32),
            pltpu.VMEM((4, UNIT, E), F32),
            pltpu.VMEM((16, UNIT, E), F32),
            pltpu.VMEM((UNIT, E), F32),
            pltpu.VMEM((3, OWN, E), F32),
            pltpu.VMEM((3, UNIT, E), F32),
            pltpu.VMEM((OWN, E), F32),
            pltpu.VMEM((2, 8, BLK, E), BF16),
            dma((4,)), dma((2,)),
            dma((2, 8)), dma((2, 8)),
            dma((2, 4)), dma((2, 4)),
            dma((4,)), dma((16,)),
            dma((3,)), dma((1,)),
            dma((16,)), dma((4,)),
            dma((2, 4)), dma((2, 4)),
            dma((2, 4)), dma((2, 4)),
            dma((2, 4)), dma((2, 4)),
        ],
        compiler_params=pltpu.CompilerParams(
            collective_id=0, has_side_effects=True, vmem_limit_bytes=32 * 1024 * 1024
        ),
        cost_estimate=pl.CostEstimate(flops=4 * TOK * D * E, bytes_accessed=3 * 1024 * 1024, transcendentals=0),
    )(step_count, acts, grad_logits, master, moment_one, moment_two)


def solution(mesh):
    in_specs = (
        P(("seq", "rep"), None),
        P(("seq", "rep"), None),
        P("seq", None),
        P("seq", None),
        P("seq", None),
        P(),
    )
    out_specs = (P("seq", None), P("seq", None), P("seq", None), P(("seq", "rep"), None))
    return jax.shard_map(
        per_device, mesh=mesh, in_specs=in_specs, out_specs=out_specs, check_vma=False
    )
```

time: 1570 us -> 71 us (0.05)
  waiting for transfers between devices: 1530 us -> 0 us
  Pallas kernels: 0 us -> 62.1 us
    unnamed x3 -> x0, waiting for transfers between devices: 1130 us -> none
    all_gather x1 -> x0, waiting for transfers between devices: 404 us -> none  [per_device(): lax.all_gather(weight_new, 'seq', axis=0, tiled=True)]
    pallas_call x0 -> x1, Pallas kernels: none -> 62.1 us  [per_device(): pl.pallas_call(kernel, out_shape=(own, own, own, jax.ShapeDtypeStruct((TO...]
  transfers between devices with their start and end apart: 2 -> 0, of which waited for: 2 -> 0; matrix products, arithmetic and copies ran while one was open for 0% -> 0% of each run, Pallas kernels for 0% -> 0%
where the time goes in v1:
time: 71 us; the launch traced here: 70.6 us
  Pallas kernels  62.1 us (87%)
  local copies, waits for them, and re-layouts  7.27 us (10%)
  between operations  1.3 us (2%)
    pallas_call x1, Pallas kernels, per_device(): pl.pallas_call(kernel, out_shape=(own, own, own, jax.ShapeDtypeStruct((TO...  62.1 us
    unnamed x14, local copies, waits for them, and re-layouts  7.27 us

profile of v1, /device:TPU:1, one launch (start us, length us, event | category | flops | bytes accessed | tf_op | source)
XLA Modules:
  0.0 70.6 jit_solution(759319742497827563)
XLA Ops:
  1.3 0.0 copy-start
  1.3 1.9 %copy-done = bf16[256,6144]{1,0:T(8,128)(2,1)S(1)} copy-done((bf16[256,6144]{1,0:T(8,128)(2,1)S(1)}, bf16[256,6144]{1,0:T(8,128)(2,1)}, u32[]{:S(2)}) %copy-start) | copy-done | bytes 3145752
  3.2 0.0 copy-start.1
  3.2 0.8 %copy-done.1 = bf16[256,128]{1,0:T(8,128)(2,1)S(1)} copy-done((bf16[256,128]{1,0:T(8,128)(2,1)S(1)}, bf16[256,128]{1,0:T(8,128)(2,1)}, u32[]{:S(2)}) %copy-start.1) | copy-done | bytes 65560
  4.0 0.0 copy-start.2
  4.0 0.7 copy-done.2
  4.7 0.0 copy-start.3
  4.7 0.7 copy-done.3
  5.4 0.0 copy-start.4
  5.4 0.7 copy-done.4
  6.1 62.1 %shard_map.93 = (f32[24,128]{1,0:T(8,128)S(1)}, f32[24,128]{1,0:T(8,128)S(1)}, f32[24,128]{1,0:T(8,128)S(1)}, bf16[256,128]{1,0:T(8,128)(2,1)S(1)}) custom-call(s32[1]{0:T(128)S(6)} %copy.14.step_ref, bf16[256,6144]{1,0:T(8,128)(2,1)S(1)} %copy-done, bf16[256,128]{1,0:T(8,128)(2,1)S(1)} %copy-done.1, f32[24,128]{1,0:T(8,128)S(1)} %copy-done.2, ...), custom_call_target="tpu_custom_call" | custom-call | flops 805306368 | bytes 3145728 | tf_op jit(solution)/shard_map/pallas_call | solution.py:290
  68.2 0.6 copy.15
  68.8 0.6 copy.16
  69.4 0.6 copy.17
  70.0 0.6 copy.18
Async XLA Ops:
  1.3 1.9 %copy-start = (bf16[256,6144]{1,0:T(8,128)(2,1)S(1)}, bf16[256,6144]{1,0:T(8,128)(2,1)}, u32[]{:S(2)}) copy-start(bf16[256,6144]{1,0:T(8,128)(2,1)} %acts_hbm.1) | copy-start | bytes 9437188
  3.2 0.8 %copy-start.1 = (bf16[256,128]{1,0:T(8,128)(2,1)S(1)}, bf16[256,128]{1,0:T(8,128)(2,1)}, u32[]{:S(2)}) copy-start(bf16[256,128]{1,0:T(8,128)(2,1)} %glog_ref.1) | copy-start | bytes 196612
  4.0 0.7 %copy-start.2 = (f32[24,128]{1,0:T(8,128)S(1)}, f32[24,128]{1,0:T(8,128)}, u32[]{:S(2)}) copy-start(f32[24,128]{1,0:T(8,128)} %master_ref.1) | copy-start | bytes 36868
  4.7 0.7 %copy-start.3 = (f32[24,128]{1,0:T(8,128)S(1)}, f32[24,128]{1,0:T(8,128)}, u32[]{:S(2)}) copy-start(f32[24,128]{1,0:T(8,128)} %one_ref.1) | copy-start | bytes 36868
  5.4 0.7 %copy-start.4 = (f32[24,128]{1,0:T(8,128)S(1)}, f32[24,128]{1,0:T(8,128)}, u32[]{:S(2)}) copy-start(f32[24,128]{1,0:T(8,128)} %two_ref.1) | copy-start | bytes 36868

commit v2 on v1

--- a/solution.py
+++ b/solution.py
@@ -16,6 +16,8 @@
 F32 = jnp.float32
 BF16 = jnp.bfloat16
 PAIRS = ((2, 0), (2, 1), (1, 0), (3, 0), (1, 1), (3, 1), (0, 1))
+STEPS = (2, 1, 3, 0)
+ORDER = (0, 1, 2, 3, 4, 5, 6, 7, 15, 14, 13, 8, 12, 9, 10, 11)
 NEAR = ((0, 1), (1, 0), (3, 0), (1, 1), (3, 1), (2, 0), (2, 1))
 
 
@@ -30,10 +32,10 @@
 
 
 def kernel(
-    step_ref, acts_hbm, glog_ref, master_ref, one_ref, two_ref,
-    master_out, one_out, two_out, logits_out,
-    acts, part, recv_a, acc, recv_b, unit, recv_c, own48, state, state48, grad_own, wnew,
-    load_sem, st_sem, sa, ra, sb, rb, sc, rc, sd, rd, sz, rz, s1, r1, s2, r2, s3, r3,
+    step_hbm, acts_hbm, glog_hbm, master_hbm, one_hbm, two_hbm,
+    grad_out, logits_out,
+    step_ref, acts, glog_ref, part, recv_a, acc, recv_b, unit, recv_c, own48, state, state48, grad_own, wnew,
+    load_sem, st_sem, ready, sa, ra, sb, rb, sc, rc, sd, rd, sz, rz, s1, r1, s2, r2, s3, r3,
 ):
     seq = lax.axis_index("seq")
     rep = lax.axis_index("rep")
@@ -54,47 +56,54 @@
     def along_z(dz):
         return dev(x, y, lax.rem(z + dz, 16), core)
 
+    def load(src, dst, number):
+        copy = pltpu.make_async_copy(src, dst, load_sem.at[number])
+        copy.start()
+        return copy
+
     barrier = pltpu.get_barrier_semaphore()
-    loads = []
+    glog_load = load(glog_hbm, glog_ref, 8)
+    loads_two = []
     for k in range(4):
-        cols = pl.ds(k * 1536, 1536)
-        load = pltpu.make_async_copy(acts_hbm.at[:, cols], acts.at[:, cols], load_sem.at[k])
-        load.start()
-        loads.append(load)
+        cols = pl.ds(k * 1536 + 768, 768)
+        loads_two.append(load(acts_hbm.at[:, cols], acts.at[:, cols], 4 + k))
+    loads_one = {}
+    for d in STEPS:
+        cols = pl.ds(pl.multiple_of(lax.rem(x + d, 4) * 1536, 128), 768)
+        loads_one[d] = load(acts_hbm.at[:, cols], acts.at[:, cols], d)
+    loads_state = [load(ref, state.at[k], 9 + k) for k, ref in enumerate((master_hbm, one_hbm, two_hbm))]
+    loads_state.append(load(step_hbm, step_ref, 12))
     for h in range(2):
         for d, e in PAIRS:
             if h == 1 and d == 0:
                 continue
             pl.semaphore_signal(barrier, inc=1, device_id=at(h, d, 0, e), device_id_type=pl.DeviceIdType.MESH)
-    for dz in range(1, 16):
-        pl.semaphore_signal(barrier, inc=1, device_id=along_z(dz), device_id_type=pl.DeviceIdType.MESH)
-
-    state[0] = master_ref[...]
-    state[1] = one_ref[...]
-    state[2] = two_ref[...]
-    half = pl.ds(pl.multiple_of(core * OWN, 8), OWN)
-    state48[:, half, :] = state[...]
-
+    mod = rep * 2 + core
+    primary = lax.rem(z, 4) == mod
+    rank = sum(jnp.where(z == place, k, 0) for k, place in enumerate(ORDER))
+    expected = 13
+    for k, place in enumerate(ORDER):
+        meets = jnp.logical_and(z != place, jnp.logical_or(primary, mod == place % 4))
+
+        @pl.when(jnp.logical_and(meets, rank < k))
+        def _():
+            pl.semaphore_signal(
+                barrier, inc=1, device_id=dev(x, y, place, core), device_id_type=pl.DeviceIdType.MESH
+            )
+        expected = expected + jnp.where(jnp.logical_and(meets, rank > k), 1, 0)
+
+    glog_load.wait()
     glog = glog_ref[...]
-    for k in range(4):
-        loads[k].wait()
-        for zg in range(4):
-            cols = pl.ds(k * 1536 + zg * BLK, BLK)
-            product = lax.dot_general(
-                acts[:, cols], glog, (((0,), (0,)), ((), ())), preferred_element_type=F32
-            ).astype(BF16)
-            for zr in range(4):
-                for ylo in range(2):
-                    piece = product[(zr * 2 + ylo) * UNIT:(zr * 2 + ylo + 1) * UNIT]
-                    py = (zr // 2) * 2 + ylo
-                    pc = zr % 2
-                    if zg < 2:
-                        part[0, k * 2 + pc, py * 96 + zg * UNIT:py * 96 + zg * UNIT + UNIT] = piece
-                    else:
-                        lo = k * 96 + (zg - 2) * UNIT
-                        part[1, py * 2 + pc, lo:lo + UNIT] = piece
-
-    pl.semaphore_wait(barrier, 28)
+
+    def pieces_of(start):
+        cols = pl.ds(start if isinstance(start, int) else pl.multiple_of(start, 128), BLK)
+        product = lax.dot_general(
+            acts[:, cols], glog, (((0,), (0,)), ((), ())), preferred_element_type=F32
+        ).astype(BF16)
+        for zr in range(4):
+            for ylo in range(2):
+                lo = (zr * 2 + ylo) * UNIT
+                yield (zr // 2) * 2 + ylo, zr % 2, product[lo:lo + UNIT]
 
     def remote(src, dst, send, recv, device):
         return pltpu.make_async_remote_copy(
@@ -104,16 +113,48 @@
 
     sent = []
     copy_a = {}
+
+    def send_a(h, d, e):
+        place = lax.rem(main[h] + d, 4) * 2 + lax.rem(core + e, 2)
+        copy = remote(
+            part.at[h, place], recv_a.at[h, d * 2 + e], sa.at[h, d * 2 + e], ra.at[h, d * 2 + e],
+            at(h, d, 0, e),
+        )
+        copy.start()
+        copy_a[h, d, e] = copy
+        sent.append(copy)
+
+    for k in range(4):
+        loads_two[k].wait()
+        for zg in range(2, 4):
+            for py, pc, piece in pieces_of(k * 1536 + zg * BLK):
+                lo = k * 96 + (zg - 2) * UNIT
+                part[1, py * 2 + pc, lo:lo + UNIT] = piece
+    pl.semaphore_wait(barrier, expected)
     for d, e in PAIRS:
-        for h in range(2):
-            place = lax.rem(main[h] + d, 4) * 2 + lax.rem(core + e, 2)
-            copy = remote(
-                part.at[h, place], recv_a.at[h, d * 2 + e], sa.at[h, d * 2 + e], ra.at[h, d * 2 + e],
-                at(h, d, 0, e),
+        send_a(1, d, e)
+    for d in STEPS:
+        loads_one[d].wait()
+        to = lax.rem(x + d, 4)
+        for zg in range(2):
+            for py, pc, piece in pieces_of(to * 1536 + zg * BLK):
+                lo = py * 96 + zg * UNIT
+                part[0, to * 2 + pc, lo:lo + UNIT] = piece
+        for p, e in PAIRS:
+            if p == d:
+                send_a(0, p, e)
+
+    for k, place in enumerate(ORDER):
+        @pl.when(jnp.logical_and(primary, rank > k))
+        def _():
+            pl.semaphore_signal(
+                ready.at[z // 4], inc=1, device_id=dev(x, y, place, core), device_id_type=pl.DeviceIdType.MESH
             )
-            copy.start()
-            copy_a[h, d, e] = copy
-            sent.append(copy)
+
+    for copy in loads_state:
+        copy.wait()
+    half = pl.ds(pl.multiple_of(core * OWN, 8), OWN)
+    state48[:, half, :] = state[...]
     state_copy = remote(state, state48.at[:, half, :], st_sem.at[0], st_sem.at[1], at(0, 0, 0, 1))
     state_copy.start()
     sent.append(state_copy)
@@ -136,8 +177,6 @@
                 copy_b[h, d] = copy
                 sent.append(copy)
 
-    mod = rep * 2 + core
-    primary = lax.rem(z, 4) == mod
     copy_c = []
     for h in range(2):
         for d in (1, 3, 2):
@@ -150,6 +189,11 @@
             dz = lax.rem(to + 16 - z, 16)
             copy = remote(unit.at[zg], recv_c.at[dz], sc.at[zg], rc.at[dz], dev(x, y, to, core))
             copy_c.append((copy, dz))
+            rank_to = sum(jnp.where(to == place, k, 0) for k, place in enumerate(ORDER))
+
+            @pl.when(rank < rank_to)
+            def _():
+                pl.semaphore_wait(ready.at[zg], 1)
 
             @pl.when(dz != 0)
             def _():
@@ -170,9 +214,9 @@
 
     zg_me = z // 4
     spot = place(zg_me // 2, lax.rem(zg_me, 2))
-    copy_z = [
-        remote(spot, spot, sz.at[dz], rz.at[zg_me], along_z(dz)) for dz in range(1, 16)
-    ]
+    copy_z = {
+        to: remote(spot, spot, sz.at[to], rz.at[zg_me], dev(x, y, to, core)) for to in range(16)
+    }
     copy_d = [
         remote(own48.at[half], grad_own, sd.at[0], rd.at[0], at(1, 2, 0, 0)),
         remote(own48.at[other], grad_own, sd.at[1], rd.at[0], at(1, 0, 0, 1)),
@@ -188,8 +232,10 @@
             total = total + recv_c[dz]
         updated, _, _ = adam(total, state48[0], state48[1], state48[2], count)
         spot[...] = updated.astype(BF16)
-        for dz in (8, 7, 9, 6, 10, 5, 11, 4, 12, 3, 13, 2, 14, 1, 15):
-            copy_z[dz - 1].start()
+        for to in (0, 1, 2, 3, 4, 15, 5, 14, 6, 13, 7, 12, 8, 11, 9, 10):
+            @pl.when(z != to)
+            def _():
+                copy_z[to].start()
         own48[...] = total
         for copy in copy_d:
             copy.start()
@@ -235,37 +281,34 @@
     def _():
         remote(grad_own, grad_own, sd.at[0], rd.at[0], at(1, 2, 0, 0)).wait_recv()
 
-    updated, first, second = adam(grad_own[...], state[0], state[1], state[2], count)
-    master_out[...] = updated
-    one_out[...] = first
-    two_out[...] = second
-
-    for d in (1, 3, 2):
-        for h in range(2):
-            copy_2[h, d].wait_recv()
-            forward(h, 4 - d)
+    grad_out[...] = grad_own[...]
+
+    total = jnp.zeros((TOK, E), F32)
     for d in (0, 1, 3, 2):
-        for h in range(2):
-            copy_3[h, d].wait_recv()
-
-    total = jnp.zeros((TOK, E), F32)
+        from_d = (4 - d) % 4
+        if d:
+            for h in range(2):
+                copy_2[h, d].wait_recv()
+                forward(h, from_d)
+        copy_3[0, from_d].wait_recv()
+        lane = lax.rem(x + from_d, 4)
+        for zg in range(2):
+            weights = [
+                wnew[0, lane * 2 + zr % 2, ((zr // 2) * 2 + ylo) * 96 + zg * UNIT:((zr // 2) * 2 + ylo) * 96 + zg * UNIT + UNIT]
+                for zr in range(4) for ylo in range(2)
+            ]
+            cols = pl.ds(pl.multiple_of(lane * 1536 + zg * BLK, 128), BLK)
+            total = total + jnp.dot(acts[:, cols], jnp.concatenate(weights, axis=0), preferred_element_type=F32)
+    for d in range(4):
+        copy_3[1, d].wait_recv()
     for k in range(4):
-        for zg in range(4):
-            pieces = []
-            for zr in range(4):
-                for ylo in range(2):
-                    py = (zr // 2) * 2 + ylo
-                    pc = zr % 2
-                    if zg < 2:
-                        lo = py * 96 + zg * UNIT
-                        pieces.append(wnew[0, k * 2 + pc, lo:lo + UNIT])
-                    else:
-                        lo = k * 96 + (zg - 2) * UNIT
-                        pieces.append(wnew[1, py * 2 + pc, lo:lo + UNIT])
-            cols = pl.ds(k * 1536 + zg * BLK, BLK)
-            total = total + jnp.dot(
-                acts[:, cols], jnp.concatenate(pieces, axis=0), preferred_element_type=F32
-            )
+        for zg in range(2):
+            weights = [
+                wnew[1, ((zr // 2) * 2 + ylo) * 2 + zr % 2, k * 96 + zg * UNIT:k * 96 + zg * UNIT + UNIT]
+                for zr in range(4) for ylo in range(2)
+            ]
+            cols = pl.ds(k * 1536 + 768 + zg * BLK, BLK)
+            total = total + jnp.dot(acts[:, cols], jnp.concatenate(weights, axis=0), preferred_element_type=F32)
     logits_out[...] = total.astype(BF16)
 
     for copy in sent:
@@ -277,25 +320,30 @@
 
     @pl.when(primary)
     def _():
-        for copy in copy_z:
-            copy.wait_send()
+        for to in range(16):
+            @pl.when(z != to)
+            def _():
+                copy_z[to].wait_send()
         for copy in copy_d:
             copy.wait_send()
 
 
 def per_device(acts, grad_logits, master, moment_one, moment_two, step_count):
     vmem = pl.BlockSpec(memory_space=pltpu.VMEM)
+    anywhere = pl.BlockSpec(memory_space=pl.ANY)
     dma = pltpu.SemaphoreType.DMA
     own = jax.ShapeDtypeStruct((OWN, E), F32)
-    return pl.pallas_call(
+    grad, logits = pl.pallas_call(
         kernel,
-        out_shape=(own, own, own, jax.ShapeDtypeStruct((TOK, E), BF16)),
+        out_shape=(own, jax.ShapeDtypeStruct((TOK, E), BF16)),
         in_specs=[
-            pl.BlockSpec(memory_space=pltpu.SMEM), pl.BlockSpec(memory_space=pl.ANY), vmem, vmem, vmem, vmem,
+            anywhere, anywhere, anywhere, anywhere, anywhere, anywhere,
         ],
-        out_specs=(vmem, vmem, vmem, vmem),
+        out_specs=(vmem, vmem),
         scratch_shapes=[
+            pltpu.SMEM((1,), jnp.int32),
             pltpu.VMEM((TOK, D), BF16),
+            pltpu.VMEM((TOK, E), BF16),
             pltpu.VMEM((2, 8, BLK, E), BF16),
             pltpu.VMEM((2, 8, BLK, E), BF16),
             pltpu.VMEM((2, 4, 96, E), F32),
@@ -307,7 +355,7 @@
             pltpu.VMEM((3, UNIT, E), F32),
             pltpu.VMEM((OWN, E), F32),
             pltpu.VMEM((2, 8, BLK, E), BF16),
-            dma((4,)), dma((2,)),
+            dma((13,)), dma((2,)), pltpu.SemaphoreType.REGULAR((4,)),
             dma((2, 8)), dma((2, 8)),
             dma((2, 4)), dma((2, 4)),
             dma((4,)), dma((16,)),
@@ -318,10 +366,17 @@
             dma((2, 4)), dma((2, 4)),
         ],
         compiler_params=pltpu.CompilerParams(
-            collective_id=0, has_side_effects=True, vmem_limit_bytes=32 * 1024 * 1024
+            collective_id=0, has_side_effects=True, vmem_limit_bytes=60 * 1024 * 1024
         ),
         cost_estimate=pl.CostEstimate(flops=4 * TOK * D * E, bytes_accessed=3 * 1024 * 1024, transcendentals=0),
     )(step_count, acts, grad_logits, master, moment_one, moment_two)
+    count = step_count[0].astype(F32)
+    first = 0.9 * moment_one + (1.0 - 0.9) * grad
+    second = 0.95 * moment_two + (1.0 - 0.95) * grad * grad
+    first_hat = first / (1.0 - jnp.power(0.9, count))
+    second_hat = second / (1.0 - jnp.power(0.95, count))
+    updated = master - 0.01 * (first_hat / (jnp.sqrt(second_hat) + 1e-08) + 0.1 * master)
+    return updated, first, second, logits
 
 
 def solution(mesh):

time: 71 us -> 65.7 us (0.925)
  local copies, waits for them, and re-layouts: 7.27 us -> 1.48 us
  other arithmetic: 0 us -> 1.34 us
  Pallas kernels: 62.1 us -> 61.2 us
    unnamed x14 -> x7, local copies, waits for them, and re-layouts: 7.27 us -> 1.48 us
    sub x0 -> x1, other arithmetic: none -> 1.34 us  [per_device(): master - 0.01 * (first_hat / (jnp.sqrt(second_hat) + 1e-08) + 0.1 * master)]
    pallas_call x1, Pallas kernels: 62.1 us -> 61.2 us  [per_device(): pl.pallas_call(kernel, out_shape=(own, jax.ShapeDtypeStruct((TOK, E), BF1...]
where the time goes in v2:
time: 65.7 us; the launch traced here: 65.5 us
  Pallas kernels  61.2 us (93%)
  local copies, waits for them, and re-layouts  1.48 us (2%)
  between operations  1.44 us (2%)
  other arithmetic  1.34 us (2%)
    pallas_call x1, Pallas kernels, per_device(): pl.pallas_call(kernel, out_shape=(own, jax.ShapeDtypeStruct((TOK, E), BF1...  61.2 us
    unnamed x7, local copies, waits for them, and re-layouts  1.48 us
    sub x1, other arithmetic, per_device(): master - 0.01 * (first_hat / (jnp.sqrt(second_hat) + 1e-08) + 0.1 * master)  1.34 us

profile of v2, /device:TPU:1, one launch (start us, length us, event | category | flops | bytes accessed | tf_op | source)
XLA Modules:
  0.0 65.5 jit_solution(14680396248948388740)
XLA Ops:
  0.6 0.0 copy-start.2
  0.6 0.0 copy-start.1
  0.7 0.0 copy-start
  1.4 61.2 %shard_map.93 = (f32[24,128]{1,0:T(8,128)}, bf16[256,128]{1,0:T(8,128)(2,1)}) custom-call(s32[1]{0:T(128)S(6)} %copy.11.step_hbm, bf16[256,6144]{1,0:T(8,128)(2,1)} %acts_hbm.1, bf16[256,128]{1,0:T(8,128)(2,1)} %glog_hbm.1, f32[24,128]{1,0:T(8,128)} %master_hbm.1, f32[24,128]{1,0:T(8,128)} %one_hbm.1, f32[24,128]{1,0:T(8,128)} %two_hbm.1), custom_call_target="tpu_custom_call" | custom-call | flops 805306368 | bytes 3145728 | tf_op jit(solution)/shard_map/pallas_call | solution.py:336
  62.6 0.0 copy-done.2
  62.6 0.0 copy-done.1
  62.7 0.0 copy-done
  62.7 1.3 %multiply_subtract_fusion = (f32[24,128]{1,0:T(8,128)}, f32[24,128]{1,0:T(8,128)}, f32[24,128]{1,0:T(8,128)}) fusion(f32[24,128]{1,0:T(8,128)S(1)} %copy-done, f32[]{:T(128)} %bitcast.1, f32[]{:T(128)} %bitcast, f32[24,128]{1,0:T(8,128)} %get-tuple-element.6, f32[24,128]{1,0:T(8,128)S(1)} %copy-done.2, f32[24,128]{1,0:T(8,128)S(1)} %copy-done.1), kind=kLoop, calls=%fused_computation.2 | loop fusion | flops 46080 | bytes 86024 | tf_op jit(solution)/shard_map/sub | solution.py:378
  64.0 1.5 %copy.12 = bf16[256,128]{1,0:T(8,128)(2,1)} copy(bf16[256,128]{1,0:T(8,128)(2,1)} %get-tuple-element.18) | data formatting | bytes 131072
Async XLA Ops:
  0.6 62.0 %copy-start.2 = (f32[24,128]{1,0:T(8,128)S(1)}, f32[24,128]{1,0:T(8,128)}, u32[]{:S(2)}) copy-start(f32[24,128]{1,0:T(8,128)} %two_hbm.1) | copy-start | bytes 36868
  0.6 62.0 %copy-start.1 = (f32[24,128]{1,0:T(8,128)S(1)}, f32[24,128]{1,0:T(8,128)}, u32[]{:S(2)}) copy-start(f32[24,128]{1,0:T(8,128)} %one_hbm.1) | copy-start | bytes 36868
  0.7 62.0 %copy-start = (f32[24,128]{1,0:T(8,128)S(1)}, f32[24,128]{1,0:T(8,128)}, u32[]{:S(2)}) copy-start(f32[24,128]{1,0:T(8,128)} %master_hbm.1) | copy-start | bytes 36868

commit v3 on v2

v3 whole, which is shorter than its diff:
```python
import math

import jax
import jax.numpy as jnp
from jax import lax
from jax.experimental import pallas as pl
from jax.experimental.pallas import tpu as pltpu
from jax.sharding import PartitionSpec as P

D = 6144
E = 128
TOK = 256
OWN = 24
UNIT = 48
BLK = 384
F32 = jnp.float32
BF16 = jnp.bfloat16
PAIRS = ((2, 0), (2, 1), (1, 0), (3, 0), (1, 1), (3, 1), (0, 1))
STEPS = (2, 1, 3, 0)
CHUNKS = ((1, 0), (0, 1), (1, 1), (0, 0))
ORDER = (0, 1, 2, 3, 4, 5, 6, 7, 15, 14, 13, 8, 12, 9, 10, 11)
NEAR = ((0, 1), (1, 0), (3, 0), (1, 1), (3, 1), (2, 0), (2, 1))


def adam(grad, master, one, two, count):
    ones = jnp.ones((1, E), F32)
    first = 0.9 * one + (1.0 - 0.9) * grad
    second = 0.95 * two + (1.0 - 0.95) * grad * grad
    first_hat = first / (1.0 - jnp.exp(count * math.log(0.9) * ones))
    second_hat = second / (1.0 - jnp.exp(count * math.log(0.95) * ones))
    updated = master - 0.01 * (first_hat / (jnp.sqrt(second_hat) + 1e-08) + 0.1 * master)
    return updated, first, second


def kernel(
    step_hbm, acts_hbm, glog_hbm, master_hbm, one_hbm, two_hbm,
    grad_out, logits_out,
    step_ref, acts, glog_ref, part, recv_a, acc, recv_b, unit, recv_c, own48, state, state48, grad_own, wnew,
    load_sem, st_sem, ready, sa, ra, sb, rb, sc, rc, sd, rd, sz, rz, s1, r1, s2, r2, s3, r3,
):
    seq = lax.axis_index("seq")
    rep = lax.axis_index("rep")
    core = lax.rem(seq, 2)
    y = rep * 2 + lax.rem(seq // 2, 2)
    z = lax.rem(seq // 4, 16)
    x = seq // 64
    main = (x, y)
    cross = (y, x)

    def dev(px, py, pz, pc):
        return {"seq": ((px * 16 + pz) * 2 + lax.rem(py, 2)) * 2 + pc, "rep": py // 2}

    def at(h, dmain, dcross, dcore):
        dx, dy = (dmain, dcross) if h == 0 else (dcross, dmain)
        return dev(lax.rem(x + dx, 4), lax.rem(y + dy, 4), z, lax.rem(core + dcore, 2))

    def along_z(dz):
        return dev(x, y, lax.rem(z + dz, 16), core)

    def block(h, k, d):
        start = lax.rem(x + d, 4) * 1536 + (h * 2 + k) * BLK
        return pl.ds(pl.multiple_of(start, 128), BLK)

    def load(src, dst, number):
        copy = pltpu.make_async_copy(src, dst, load_sem.at[number])
        copy.start()
        return copy

    barrier = pltpu.get_barrier_semaphore()
    glog_load = load(glog_hbm, glog_ref, 16)
    loads = {}
    for h, k in CHUNKS:
        for d in STEPS:
            cols = block(h, k, d)
            loads[h, k, d] = load(acts_hbm.at[:, cols], acts.at[:, cols], (h * 2 + k) * 4 + d)
    loads_state = [load(ref, state.at[k], 17 + k) for k, ref in enumerate((master_hbm, one_hbm, two_hbm))]
    loads_state.append(load(step_hbm, step_ref, 20))
    for h in range(2):
        for d, e in PAIRS:
            if h == 1 and d == 0:
                continue
            pl.semaphore_signal(barrier, inc=1, device_id=at(h, d, 0, e), device_id_type=pl.DeviceIdType.MESH)
    mod = rep * 2 + core
    primary = lax.rem(z, 4) == mod
    rank = sum(jnp.where(z == place, k, 0) for k, place in enumerate(ORDER))
    expected = 13
    for k, place in enumerate(ORDER):
        meets = jnp.logical_and(z != place, jnp.logical_or(primary, mod == place % 4))

        @pl.when(jnp.logical_and(meets, rank < k))
        def _():
            pl.semaphore_signal(
                barrier, inc=1, device_id=dev(x, y, place, core), device_id_type=pl.DeviceIdType.MESH
            )
        expected = expected + jnp.where(jnp.logical_and(meets, rank > k), 1, 0)

    glog_load.wait()
    glog = glog_ref[...]

    def remote(src, dst, send, recv, device):
        return pltpu.make_async_remote_copy(
            src_ref=src, dst_ref=dst, send_sem=send, recv_sem=recv,
            device_id=device, device_id_type=pl.DeviceIdType.MESH,
        )

    sent = []
    copy_a = {}

    def send_a(h, k, d, e):
        q = h * 2 + k
        place = lax.rem(main[h] + d, 4) * 2 + lax.rem(core + e, 2)
        copy = remote(
            part.at[q, place], recv_a.at[q, d * 2 + e], sa.at[q, d * 2 + e], ra.at[q, d * 2 + e], at(h, d, 0, e)
        )
        copy.start()
        copy_a[h, k, d, e] = copy
        sent.append(copy)

    for h, k in CHUNKS:
        q = h * 2 + k
        for d in STEPS:
            to = lax.rem(x + d, 4)
            loads[h, k, d].wait()
            product = lax.dot_general(
                acts[:, block(h, k, d)], glog, (((0,), (0,)), ((), ())), preferred_element_type=F32
            ).astype(BF16)
            for zr in range(4):
                for ylo in range(2):
                    lo = (zr * 2 + ylo) * UNIT
                    py, pc = (zr // 2) * 2 + ylo, zr % 2
                    if h == 0:
                        part[q, to * 2 + pc, py * UNIT:(py + 1) * UNIT] = product[lo:lo + UNIT]
                    else:
                        part[q, py * 2 + pc, pl.ds(pl.multiple_of(to * UNIT, 16), UNIT)] = product[lo:lo + UNIT]
            if h == 0:
                for p, e in PAIRS:
                    if p == d:
                        send_a(h, k, p, e)
        if h == 1:
            if (h, k) == CHUNKS[0]:
                pl.semaphore_wait(barrier, expected)
            for d, e in PAIRS:
                send_a(h, k, d, e)
    for k, place in enumerate(ORDER):
        @pl.when(jnp.logical_and(primary, rank > k))
        def _():
            pl.semaphore_signal(
                ready.at[z // 4], inc=1, device_id=dev(x, y, place, core), device_id_type=pl.DeviceIdType.MESH
            )

    for copy in loads_state:
        copy.wait()
    half = pl.ds(pl.multiple_of(core * OWN, 8), OWN)
    state48[:, half, :] = state[...]
    state_copy = remote(state, state48.at[:, half, :], st_sem.at[0], st_sem.at[1], at(0, 0, 0, 1))
    state_copy.start()
    sent.append(state_copy)

    copy_b = {}
    for h, k in CHUNKS:
        q = h * 2 + k
        mine = main[h] * 2 + core
        for d, e in NEAR:
            copy_a[h, k, d, e].wait_recv()
        for d in (2, 1, 3, 0):
            to = lax.rem(cross[h] + d, 4)
            rows = pl.ds(pl.multiple_of(to * UNIT, 16), UNIT)
            total = part[q, mine, rows].astype(F32)
            for p, e in NEAR:
                total = total + recv_a[q, p * 2 + e, rows].astype(F32)
            acc[q, d] = total
            if d:
                copy = remote(acc.at[q, d], recv_b.at[q, d], sb.at[q, d], rb.at[q, d], at(h, 0, d, 0))
                copy.start()
                copy_b[h, k, d] = copy
                sent.append(copy)

    copy_c = []
    for h, k in CHUNKS:
        zg = h * 2 + k
        for d in (1, 3, 2):
            copy_b[h, k, d].wait_recv()
        unit[zg] = ((acc[zg, 0] + recv_b[zg, 1]) + recv_b[zg, 3]) + recv_b[zg, 2]
        to = zg * 4 + mod
        dz = lax.rem(to + 16 - z, 16)
        copy = remote(unit.at[zg], recv_c.at[dz], sc.at[zg], rc.at[dz], dev(x, y, to, core))
        copy_c.append((copy, dz))
        rank_to = sum(jnp.where(to == place, j, 0) for j, place in enumerate(ORDER))

        @pl.when(rank < rank_to)
        def _():
            pl.semaphore_wait(ready.at[zg], 1)

        @pl.when(dz != 0)
        def _():
            copy.start()

        @pl.when(dz == 0)
        def _():
            own48[...] = unit[zg]

    count = step_ref[0].astype(F32)
    state_copy.wait_recv()
    other = pl.ds(pl.multiple_of((1 - core) * OWN, 8), OWN)

    def place(zg):
        first = zg // 2 == 0
        which = jnp.where(first, x, y)
        inner = jnp.where(first, y, x)
        return wnew.at[zg, which * 2 + core, pl.ds(pl.multiple_of(inner * UNIT, 16), UNIT)]

    zg_me = z // 4
    spot = place(zg_me)
    copy_z = {
        to: remote(spot, spot, sz.at[to], rz.at[zg_me], dev(x, y, to, core)) for to in range(16)
    }
    copy_d = [
        remote(own48.at[half], grad_own, sd.at[0], rd.at[0], at(1, 2, 0, 0)),
        remote(own48.at[other], grad_own, sd.at[1], rd.at[0], at(1, 0, 0, 1)),
        remote(own48.at[other], grad_own, sd.at[2], rd.at[0], at(1, 2, 0, 1)),
    ]

    @pl.when(primary)
    def _():
        for dz in range(1, 16):
            remote(recv_c.at[dz], recv_c.at[dz], sc.at[0], rc.at[dz], along_z(dz)).wait_recv()
        total = own48[...]
        for dz in range(1, 16):
            total = total + recv_c[dz]
        updated, _, _ = adam(total, state48[0], state48[1], state48[2], count)
        spot[...] = updated.astype(BF16)
        for to in (0, 1, 2, 3, 4, 15, 5, 14, 6, 13, 7, 12, 8, 11, 9, 10):
            @pl.when(z != to)
            def _():
                copy_z[to].start()
        own48[...] = total
        for copy in copy_d:
            copy.start()
        grad_own[...] = own48[half]

    copy_1 = {}
    for h, k in CHUNKS:
        zg = h * 2 + k

        @pl.when(z != zg * 4 + mod)
        def _():
            remote(place(zg), place(zg), sz.at[0], rz.at[zg], along_z(1)).wait_recv()
        for d in (2, 1, 3):
            copy = remote(place(zg), place(zg), s1.at[zg, d], r1.at[zg, d], at(h, 0, d, 0))
            copy.start()
            copy_1[h, k, d] = copy
            sent.append(copy)

    copy_2 = {}
    copy_3 = {}

    def forward(h, k, d):
        q = h * 2 + k
        lane = wnew.at[q, lax.rem(main[h] + d, 4) * 2 + core]
        copy = remote(lane, lane, s3.at[q, d], r3.at[q, d], at(h, 0, 0, 1))
        copy.start()
        copy_3[h, k, d] = copy
        sent.append(copy)

    for h, k in CHUNKS:
        q = h * 2 + k
        for d in (1, 3, 2):
            copy_1[h, k, d].wait_recv()
        mine = wnew.at[q, main[h] * 2 + core]
        for d in (2, 1, 3):
            copy = remote(mine, mine, s2.at[q, d], r2.at[q, d], at(h, d, 0, 0))
            copy.start()
            copy_2[h, k, d] = copy
            sent.append(copy)
        forward(h, k, 0)

    @pl.when(jnp.logical_not(primary))
    def _():
        remote(grad_own, grad_own, sd.at[0], rd.at[0], at(1, 2, 0, 0)).wait_recv()

    grad_out[...] = grad_own[...]

    logits = jnp.zeros((TOK, E), F32)

    def apply(total, h, k):
        q = h * 2 + k
        for d in range(4):
            copy_3[h, k, d].wait_recv()
        for lane in range(4):
            weights = []
            for zr in range(4):
                for ylo in range(2):
                    py, pc = (zr // 2) * 2 + ylo, zr % 2
                    which, inner = (lane, py) if h == 0 else (py, lane)
                    weights.append(wnew[q, which * 2 + pc, inner * UNIT:(inner + 1) * UNIT])
            cols = pl.ds(lane * 1536 + q * BLK, BLK)
            total = total + jnp.dot(acts[:, cols], jnp.concatenate(weights, axis=0), preferred_element_type=F32)
        return total

    for number, (h, k) in enumerate(CHUNKS):
        for d in (1, 3, 2):
            copy_2[h, k, d].wait_recv()
            forward(h, k, 4 - d)
        if number:
            logits = apply(logits, *CHUNKS[number - 1])
    logits = apply(logits, *CHUNKS[-1])
    logits_out[...] = logits.astype(BF16)

    for copy in sent:
        copy.wait_send()
    for copy, dz in copy_c:
        @pl.when(dz != 0)
        def _():
            copy.wait_send()

    @pl.when(primary)
    def _():
        for to in range(16):
            @pl.when(z != to)
            def _():
                copy_z[to].wait_send()
        for copy in copy_d:
            copy.wait_send()


def per_device(acts, grad_logits, master, moment_one, moment_two, step_count):
    vmem = pl.BlockSpec(memory_space=pltpu.VMEM)
    anywhere = pl.BlockSpec(memory_space=pl.ANY)
    dma = pltpu.SemaphoreType.DMA
    own = jax.ShapeDtypeStruct((OWN, E), F32)
    grad, logits = pl.pallas_call(
        kernel,
        out_shape=(pltpu.VMEM((OWN, E), F32), pltpu.VMEM((TOK, E), BF16)),
        in_specs=[
            anywhere, anywhere, anywhere, anywhere, anywhere, anywhere,
        ],
        out_specs=(vmem, vmem),
        scratch_shapes=[
            pltpu.SMEM((1,), jnp.int32),
            pltpu.VMEM((TOK, D), BF16),
            pltpu.VMEM((TOK, E), BF16),
            pltpu.VMEM((4, 8, 4 * UNIT, E), BF16),
            pltpu.VMEM((4, 8, 4 * UNIT, E), BF16),
            pltpu.VMEM((4, 4, UNIT, E), F32),
            pltpu.VMEM((4, 4, UNIT, E), F32),
            pltpu.VMEM((4, UNIT, E), F32),
            pltpu.VMEM((16, UNIT, E), F32),
            pltpu.VMEM((UNIT, E), F32),
            pltpu.VMEM((3, OWN, E), F32),
            pltpu.VMEM((3, UNIT, E), F32),
            pltpu.VMEM((OWN, E), F32),
            pltpu.VMEM((4, 8, 4 * UNIT, E), BF16),
            dma((21,)), dma((2,)), pltpu.SemaphoreType.REGULAR((4,)),
            dma((4, 8)), dma((4, 8)),
            dma((4, 4)), dma((4, 4)),
            dma((4,)), dma((16,)),
            dma((3,)), dma((1,)),
            dma((16,)), dma((4,)),
            dma((4, 4)), dma((4, 4)),
            dma((4, 4)), dma((4, 4)),
            dma((4, 4)), dma((4, 4)),
        ],
        compiler_params=pltpu.CompilerParams(
            collective_id=0, has_side_effects=True, vmem_limit_bytes=60 * 1024 * 1024
        ),
        cost_estimate=pl.CostEstimate(flops=4 * TOK * D * E, bytes_accessed=3 * 1024 * 1024, transcendentals=0),
    )(step_count, acts, grad_logits, master, moment_one, moment_two)
    count = step_count[0].astype(F32)
    first = 0.9 * moment_one + (1.0 - 0.9) * grad
    second = 0.95 * moment_two + (1.0 - 0.95) * grad * grad
    first_hat = first / (1.0 - jnp.power(0.9, count))
    second_hat = second / (1.0 - jnp.power(0.95, count))
    updated = master - 0.01 * (first_hat / (jnp.sqrt(second_hat) + 1e-08) + 0.1 * master)
    return updated, first, second, logits


def solution(mesh):
    in_specs = (
        P(("seq", "rep"), None),
        P(("seq", "rep"), None),
        P("seq", None),
        P("seq", None),
        P("seq", None),
        P(),
    )
    out_specs = (P("seq", None), P("seq", None), P("seq", None), P(("seq", "rep"), None))
    return jax.shard_map(
        per_device, mesh=mesh, in_specs=in_specs, out_specs=out_specs, check_vma=False
    )
```

time: 65.7 us -> 58.4 us (0.89)
  Pallas kernels: 61.2 us -> 55.6 us
  local copies, waits for them, and re-layouts: 1.48 us -> 0.64 us
  other arithmetic: 1.34 us -> 0.64 us
    pallas_call x1, Pallas kernels: 61.2 us -> 55.6 us  [per_device(): pl.pallas_call(kernel, out_shape=(pltpu.VMEM((OWN, E), F32), pltpu.VMEM((...]
    unnamed x7, local copies, waits for them, and re-layouts: 1.48 us -> 0.64 us
    sub x1, other arithmetic: 1.34 us -> 0.64 us  [per_device(): master - 0.01 * (first_hat / (jnp.sqrt(second_hat) + 1e-08) + 0.1 * master)]
where the time goes in v3:
time: 58.4 us; the launch traced here: 58.3 us
  Pallas kernels  55.6 us (95%)
  between operations  1.44 us (2%)
  local copies, waits for them, and re-layouts  0.64 us (1%)
  other arithmetic  0.64 us (1%)
    pallas_call x1, Pallas kernels, per_device(): pl.pallas_call(kernel, out_shape=(pltpu.VMEM((OWN, E), F32), pltpu.VMEM((...  55.6 us

profile of v3, /device:TPU:1, one launch (start us, length us, event | category | flops | bytes accessed | tf_op | source)
XLA Modules:
  0.0 58.3 jit_solution(15286169377436322576)
XLA Ops:
  0.6 0.0 copy-start.2
  0.6 0.0 copy-start.1
  0.7 0.0 copy-start
  1.4 55.6 %shard_map.93 = (f32[24,128]{1,0:T(8,128)S(1)}, bf16[256,128]{1,0:T(8,128)(2,1)S(1)}) custom-call(s32[1]{0:T(128)S(6)} %copy.12.step_hbm, bf16[256,6144]{1,0:T(8,128)(2,1)} %acts_hbm.1, bf16[256,128]{1,0:T(8,128)(2,1)} %glog_hbm.1, f32[24,128]{1,0:T(8,128)} %master_hbm.1, f32[24,128]{1,0:T(8,128)} %one_hbm.1, f32[24,128]{1,0:T(8,128)} %two_hbm.1), custom_call_target="tpu_custom_call" | custom-call | flops 805306368 | bytes 3145728 | tf_op jit(solution)/shard_map/pallas_call | solution.py:331
  57.0 0.0 copy-done.2
  57.0 0.0 copy-done.1
  57.0 0.0 copy-done
  57.0 0.6 %multiply_subtract_fusion = (f32[24,128]{1,0:T(8,128)}, f32[24,128]{1,0:T(8,128)}, f32[24,128]{1,0:T(8,128)}) fusion(f32[24,128]{1,0:T(8,128)S(1)} %copy-done, f32[]{:T(128)} %bitcast.1, f32[]{:T(128)} %bitcast, f32[24,128]{1,0:T(8,128)S(1)} %get-tuple-element.6, f32[24,128]{1,0:T(8,128)S(1)} %copy-done.2, f32[24,128]{1,0:T(8,128)S(1)} %copy-done.1), kind=kLoop, calls=%fused_computation.2 | loop fusion | flops 46080 | bytes 86024 | tf_op jit(solution)/shard_map/sub | solution.py:373
  57.6 0.6 %copy.11 = bf16[256,128]{1,0:T(8,128)(2,1)} copy(bf16[256,128]{1,0:T(8,128)(2,1)S(1)} %get-tuple-element.14) | data formatting | bytes 131072
Async XLA Ops:
  0.6 56.4 %copy-start.2 = (f32[24,128]{1,0:T(8,128)S(1)}, f32[24,128]{1,0:T(8,128)}, u32[]{:S(2)}) copy-start(f32[24,128]{1,0:T(8,128)} %two_hbm.1) | copy-start | bytes 36868
  0.6 56.4 %copy-start.1 = (f32[24,128]{1,0:T(8,128)S(1)}, f32[24,128]{1,0:T(8,128)}, u32[]{:S(2)}) copy-start(f32[24,128]{1,0:T(8,128)} %one_hbm.1) | copy-start | bytes 36868
  0.7 56.4 %copy-start = (f32[24,128]{1,0:T(8,128)S(1)}, f32[24,128]{1,0:T(8,128)}, u32[]{:S(2)}) copy-start(f32[24,128]{1,0:T(8,128)} %master_hbm.1) | copy-start | bytes 36868

commit v4 on v3

--- a/solution.py
+++ b/solution.py
@@ -12,22 +12,45 @@
 TOK = 256
 OWN = 24
 UNIT = 48
+LEVELS = 32767.0
+ROWS = 4 * UNIT
 BLK = 384
 F32 = jnp.float32
 BF16 = jnp.bfloat16
-PAIRS = ((2, 0), (2, 1), (1, 0), (3, 0), (1, 1), (3, 1), (0, 1))
+PARTNERS = ((0, 2, 0), (0, 1, 0), (0, 3, 0), (1, 2, 0), (1, 1, 0), (1, 3, 0), (1, 2, 1), (1, 0, 1))
 STEPS = (2, 1, 3, 0)
 CHUNKS = ((1, 0), (0, 1), (1, 1), (0, 0))
+GATHER = ((1, 0), (0, 1), (1, 1), (0, 0))
+ORDER = (0, 1, 2, 3, 4, 5, 6, 7, 15, 14, 13, 8, 12, 9, 10, 11)
+STEPS = (2, 1, 3, 0)
+CHUNKS = ((1, 0), (0, 1), (1, 1), (0, 0))
+GATHER = ((1, 0), (0, 1), (1, 1), (0, 0))
 ORDER = (0, 1, 2, 3, 4, 5, 6, 7, 15, 14, 13, 8, 12, 9, 10, 11)
 NEAR = ((0, 1), (1, 0), (3, 0), (1, 1), (3, 1), (2, 0), (2, 1))
 
 
-def adam(grad, master, one, two, count):
+def corrections(count):
     ones = jnp.ones((1, E), F32)
+    return 1.0 - jnp.exp(count * math.log(0.9) * ones), 1.0 - jnp.exp(count * math.log(0.95) * ones)
+
+
+def encode(total):
+    most = jnp.max(jnp.abs(total), axis=0, keepdims=True)
+    power = jnp.ceil(jnp.log2(jnp.maximum(most, 1e-30)))
+    scaled = jnp.clip(total * (LEVELS * jnp.exp2(-power)), -LEVELS, LEVELS)
+    codes = jnp.floor(scaled + 0.5).astype(jnp.int32).astype(jnp.int16)
+    return codes, jnp.broadcast_to(power.astype(jnp.int32), (16, E)).astype(jnp.int16)
+
+
+def decode_unit(powers):
+    return jnp.exp2(powers.astype(jnp.int32).astype(F32)[:1]) * (1.0 / LEVELS)
+
+
+def adam(grad, master, one, two, correction_one, correction_two):
     first = 0.9 * one + (1.0 - 0.9) * grad
     second = 0.95 * two + (1.0 - 0.95) * grad * grad
-    first_hat = first / (1.0 - jnp.exp(count * math.log(0.9) * ones))
-    second_hat = second / (1.0 - jnp.exp(count * math.log(0.95) * ones))
+    first_hat = first / correction_one
+    second_hat = second / correction_two
     updated = master - 0.01 * (first_hat / (jnp.sqrt(second_hat) + 1e-08) + 0.1 * master)
     return updated, first, second
 
@@ -35,8 +58,8 @@
 def kernel(
     step_hbm, acts_hbm, glog_hbm, master_hbm, one_hbm, two_hbm,
     grad_out, logits_out,
-    step_ref, acts, glog_ref, part, recv_a, acc, recv_b, unit, recv_c, own48, state, state48, grad_own, wnew,
-    load_sem, st_sem, ready, sa, ra, sb, rb, sc, rc, sd, rd, sz, rz, s1, r1, s2, r2, s3, r3,
+    step_ref, acts, glog_ref, part, pair, code, recv_a, acc, recv_b, unit, recv_c, own48, state, state48, grad_own, wnew,
+    load_sem, st_sem, ready, s0, r0, sa, ra, sb, rb, sc, rc, sd, rd, sz, rz, s1, r1, s2, r2, s3, r3,
 ):
     seq = lax.axis_index("seq")
     rep = lax.axis_index("rep")
@@ -57,33 +80,25 @@
     def along_z(dz):
         return dev(x, y, lax.rem(z + dz, 16), core)
 
-    def block(h, k, d):
-        start = lax.rem(x + d, 4) * 1536 + (h * 2 + k) * BLK
-        return pl.ds(pl.multiple_of(start, 128), BLK)
-
     def load(src, dst, number):
         copy = pltpu.make_async_copy(src, dst, load_sem.at[number])
         copy.start()
         return copy
 
     barrier = pltpu.get_barrier_semaphore()
+    for h, d, e in PARTNERS:
+        pl.semaphore_signal(barrier, inc=1, device_id=at(h, d, 0, e), device_id_type=pl.DeviceIdType.MESH)
     glog_load = load(glog_hbm, glog_ref, 16)
-    loads = {}
-    for h, k in CHUNKS:
-        for d in STEPS:
-            cols = block(h, k, d)
-            loads[h, k, d] = load(acts_hbm.at[:, cols], acts.at[:, cols], (h * 2 + k) * 4 + d)
+    loads = []
+    for k in range(4):
+        cols = pl.ds(k * 1536, 1536)
+        loads.append(load(acts_hbm.at[:, cols], acts.at[:, cols], k))
     loads_state = [load(ref, state.at[k], 17 + k) for k, ref in enumerate((master_hbm, one_hbm, two_hbm))]
     loads_state.append(load(step_hbm, step_ref, 20))
-    for h in range(2):
-        for d, e in PAIRS:
-            if h == 1 and d == 0:
-                continue
-            pl.semaphore_signal(barrier, inc=1, device_id=at(h, d, 0, e), device_id_type=pl.DeviceIdType.MESH)
     mod = rep * 2 + core
     primary = lax.rem(z, 4) == mod
     rank = sum(jnp.where(z == place, k, 0) for k, place in enumerate(ORDER))
-    expected = 13
+    expected = len(PARTNERS)
     for k, place in enumerate(ORDER):
         meets = jnp.logical_and(z != place, jnp.logical_or(primary, mod == place % 4))
 
@@ -103,44 +118,48 @@
             device_id=device, device_id_type=pl.DeviceIdType.MESH,
         )
 
-    sent = []
-    copy_a = {}
-
-    def send_a(h, k, d, e):
-        q = h * 2 + k
-        place = lax.rem(main[h] + d, 4) * 2 + lax.rem(core + e, 2)
-        copy = remote(
-            part.at[q, place], recv_a.at[q, d * 2 + e], sa.at[q, d * 2 + e], ra.at[q, d * 2 + e], at(h, d, 0, e)
-        )
-        copy.start()
-        copy_a[h, k, d, e] = copy
-        sent.append(copy)
-
+    for copy in loads:
+        copy.wait()
     for h, k in CHUNKS:
         q = h * 2 + k
-        for d in STEPS:
-            to = lax.rem(x + d, 4)
-            loads[h, k, d].wait()
+        for px in range(4):
+            cols = pl.ds(px * 1536 + q * BLK, BLK)
             product = lax.dot_general(
-                acts[:, block(h, k, d)], glog, (((0,), (0,)), ((), ())), preferred_element_type=F32
-            ).astype(BF16)
+                glog, acts[:, cols], (((0,), (0,)), ((), ())), preferred_element_type=F32
+            ).T.astype(BF16)
             for zr in range(4):
                 for ylo in range(2):
                     lo = (zr * 2 + ylo) * UNIT
                     py, pc = (zr // 2) * 2 + ylo, zr % 2
-                    if h == 0:
-                        part[q, to * 2 + pc, py * UNIT:(py + 1) * UNIT] = product[lo:lo + UNIT]
-                    else:
-                        part[q, py * 2 + pc, pl.ds(pl.multiple_of(to * UNIT, 16), UNIT)] = product[lo:lo + UNIT]
-            if h == 0:
-                for p, e in PAIRS:
-                    if p == d:
-                        send_a(h, k, p, e)
-        if h == 1:
-            if (h, k) == CHUNKS[0]:
-                pl.semaphore_wait(barrier, expected)
-            for d, e in PAIRS:
-                send_a(h, k, d, e)
+                    which, inner = (px, py) if h == 0 else (py, px)
+                    part[q, which * 2 + pc, inner * UNIT:(inner + 1) * UNIT] = product[lo:lo + UNIT]
+
+    sent = []
+    copy_0 = {}
+    copy_a = {}
+    pl.semaphore_wait(barrier, expected)
+    for h, k in CHUNKS:
+        q = h * 2 + k
+        for d in STEPS:
+            lane = lax.rem(main[h] + d, 4)
+            copy = remote(
+                part.at[q, lane * 2 + 1 - core], pair.at[q, d], s0.at[q, d], r0.at[q, d], at(h, 0, 0, 1)
+            )
+            copy.start()
+            copy_0[h, k, d] = copy
+            sent.append(copy)
+    for h, k in CHUNKS:
+        q = h * 2 + k
+        for d in STEPS:
+            copy_0[h, k, d].wait_recv()
+        for d in (2, 1, 3):
+            total = part[q, lax.rem(main[h] + d, 4) * 2 + core].astype(F32) + pair[q, d].astype(F32)
+            code[q, d, :ROWS], code[q, d, ROWS:] = encode(total)
+        for d in (2, 1, 3):
+            copy = remote(code.at[q, d], recv_a.at[q, d], sa.at[q, d], ra.at[q, d], at(h, d, 0, 0))
+            copy.start()
+            copy_a[h, k, d] = copy
+            sent.append(copy)
     for k, place in enumerate(ORDER):
         @pl.when(jnp.logical_and(primary, rank > k))
         def _():
@@ -160,15 +179,17 @@
     for h, k in CHUNKS:
         q = h * 2 + k
         mine = main[h] * 2 + core
-        for d, e in NEAR:
-            copy_a[h, k, d, e].wait_recv()
+        for d in (1, 3, 2):
+            copy_a[h, k, d].wait_recv()
+        units = {d: decode_unit(recv_a[q, d, ROWS:]) for d in (1, 3, 2)}
         for d in (2, 1, 3, 0):
             to = lax.rem(cross[h] + d, 4)
             rows = pl.ds(pl.multiple_of(to * UNIT, 16), UNIT)
-            total = part[q, mine, rows].astype(F32)
-            for p, e in NEAR:
-                total = total + recv_a[q, p * 2 + e, rows].astype(F32)
+            total = part[q, mine, rows].astype(F32) + pair[q, 0, rows].astype(F32)
+            for p in (1, 3, 2):
+                total = total + recv_a[q, p, rows].astype(jnp.int32).astype(F32) * units[p]
             acc[q, d] = total
+        for d in (2, 1, 3, 0):
             if d:
                 copy = remote(acc.at[q, d], recv_b.at[q, d], sb.at[q, d], rb.at[q, d], at(h, 0, d, 0))
                 copy.start()
@@ -183,7 +204,7 @@
         unit[zg] = ((acc[zg, 0] + recv_b[zg, 1]) + recv_b[zg, 3]) + recv_b[zg, 2]
         to = zg * 4 + mod
         dz = lax.rem(to + 16 - z, 16)
-        copy = remote(unit.at[zg], recv_c.at[dz], sc.at[zg], rc.at[dz], dev(x, y, to, core))
+        copy = remote(unit.at[zg], recv_c.at[z], sc.at[zg], rc.at[z], dev(x, y, to, core))
         copy_c.append((copy, dz))
         rank_to = sum(jnp.where(to == place, j, 0) for j, place in enumerate(ORDER))
 
@@ -199,8 +220,11 @@
         def _():
             own48[...] = unit[zg]
 
-    count = step_ref[0].astype(F32)
+    scales = corrections(step_ref[0].astype(F32))
     state_copy.wait_recv()
+    for copy in sent:
+        copy.wait_send()
+    sent = []
     other = pl.ds(pl.multiple_of((1 - core) * OWN, 8), OWN)
 
     def place(zg):
@@ -222,12 +246,14 @@
 
     @pl.when(primary)
     def _():
-        for dz in range(1, 16):
-            remote(recv_c.at[dz], recv_c.at[dz], sc.at[0], rc.at[dz], along_z(dz)).wait_recv()
-        total = own48[...]
-        for dz in range(1, 16):
-            total = total + recv_c[dz]
-        updated, _, _ = adam(total, state48[0], state48[1], state48[2], count)
+        recv_c[z] = own48[...]
+        total = jnp.zeros((UNIT, E), F32)
+        for place in ORDER:
+            @pl.when(z != place)
+            def _():
+                remote(recv_c.at[place], recv_c.at[place], sc.at[0], rc.at[place], along_z(1)).wait_recv()
+            total = total + recv_c[place]
+        updated, _, _ = adam(total, state48[0], state48[1], state48[2], *scales)
         spot[...] = updated.astype(BF16)
         for to in (0, 1, 2, 3, 4, 15, 5, 14, 6, 13, 7, 12, 8, 11, 9, 10):
             @pl.when(z != to)
@@ -239,7 +265,7 @@
         grad_own[...] = own48[half]
 
     copy_1 = {}
-    for h, k in CHUNKS:
+    for h, k in GATHER:
         zg = h * 2 + k
 
         @pl.when(z != zg * 4 + mod)
@@ -250,6 +276,11 @@
             copy.start()
             copy_1[h, k, d] = copy
             sent.append(copy)
+
+    for copy, dz in copy_c:
+        @pl.when(dz != 0)
+        def _():
+            copy.wait_send()
 
     copy_2 = {}
     copy_3 = {}
@@ -262,7 +293,7 @@
         copy_3[h, k, d] = copy
         sent.append(copy)
 
-    for h, k in CHUNKS:
+    for h, k in GATHER:
         q = h * 2 + k
         for d in (1, 3, 2):
             copy_1[h, k, d].wait_recv()
@@ -279,6 +310,15 @@
         remote(grad_own, grad_own, sd.at[0], rd.at[0], at(1, 2, 0, 0)).wait_recv()
 
     grad_out[...] = grad_own[...]
+
+    @pl.when(primary)
+    def _():
+        for to in range(16):
+            @pl.when(z != to)
+            def _():
+                copy_z[to].wait_send()
+        for copy in copy_d:
+            copy.wait_send()
 
     logits = jnp.zeros((TOK, E), F32)
 
@@ -297,30 +337,17 @@
             total = total + jnp.dot(acts[:, cols], jnp.concatenate(weights, axis=0), preferred_element_type=F32)
         return total
 
-    for number, (h, k) in enumerate(CHUNKS):
+    for number, (h, k) in enumerate(GATHER):
         for d in (1, 3, 2):
             copy_2[h, k, d].wait_recv()
             forward(h, k, 4 - d)
         if number:
-            logits = apply(logits, *CHUNKS[number - 1])
-    logits = apply(logits, *CHUNKS[-1])
+            logits = apply(logits, *GATHER[number - 1])
+    logits = apply(logits, *GATHER[-1])
     logits_out[...] = logits.astype(BF16)
 
     for copy in sent:
         copy.wait_send()
-    for copy, dz in copy_c:
-        @pl.when(dz != 0)
-        def _():
-            copy.wait_send()
-
-    @pl.when(primary)
-    def _():
-        for to in range(16):
-            @pl.when(z != to)
-            def _():
-                copy_z[to].wait_send()
-        for copy in copy_d:
-            copy.wait_send()
 
 
 def per_device(acts, grad_logits, master, moment_one, moment_two, step_count):
@@ -339,8 +366,10 @@
             pltpu.SMEM((1,), jnp.int32),
             pltpu.VMEM((TOK, D), BF16),
             pltpu.VMEM((TOK, E), BF16),
-            pltpu.VMEM((4, 8, 4 * UNIT, E), BF16),
-            pltpu.VMEM((4, 8, 4 * UNIT, E), BF16),
+            pltpu.VMEM((4, 8, ROWS, E), BF16),
+            pltpu.VMEM((4, 4, ROWS, E), BF16),
+            pltpu.VMEM((4, 4, ROWS + 16, E), jnp.int16),
+            pltpu.VMEM((4, 4, ROWS + 16, E), jnp.int16),
             pltpu.VMEM((4, 4, UNIT, E), F32),
             pltpu.VMEM((4, 4, UNIT, E), F32),
             pltpu.VMEM((4, UNIT, E), F32),
@@ -351,7 +380,8 @@
             pltpu.VMEM((OWN, E), F32),
             pltpu.VMEM((4, 8, 4 * UNIT, E), BF16),
             dma((21,)), dma((2,)), pltpu.SemaphoreType.REGULAR((4,)),
-            dma((4, 8)), dma((4, 8)),
+            dma((4, 4)), dma((4, 4)),
+            dma((4, 4)), dma((4, 4)),
             dma((4, 4)), dma((4, 4)),
             dma((4,)), dma((16,)),
             dma((3,)), dma((1,)),

time: 58.4 us -> 56.5 us (0.967)
  Pallas kernels: 55.6 us -> 53.6 us
    pallas_call x1, Pallas kernels: 55.6 us -> 53.6 us  [per_device(): pl.pallas_call(kernel, out_shape=(pltpu.VMEM((OWN, E), F32), pltpu.VMEM((...]
where the time goes in v4:
time: 56.5 us; the launch traced here: 56.3 us
  Pallas kernels  53.6 us (95%)
  between operations  1.44 us (3%)
  local copies, waits for them, and re-layouts  0.64 us (1%)
  other arithmetic  0.64 us (1%)
    pallas_call x1, Pallas kernels, per_device(): pl.pallas_call(kernel, out_shape=(pltpu.VMEM((OWN, E), F32), pltpu.VMEM((...  53.6 us

profile of v4, /device:TPU:1, one launch (start us, length us, event | category | flops | bytes accessed | tf_op | source)
XLA Modules:
  0.0 56.3 jit_solution(7691911203065211676)
XLA Ops:
  0.6 0.0 copy-start.2
  0.6 0.0 copy-start.1
  0.7 0.0 copy-start
  1.4 53.6 %shard_map.93 = (f32[24,128]{1,0:T(8,128)S(1)}, bf16[256,128]{1,0:T(8,128)(2,1)S(1)}) custom-call(s32[1]{0:T(128)S(6)} %copy.12.step_hbm, bf16[256,6144]{1,0:T(8,128)(2,1)} %acts_hbm.1, bf16[256,128]{1,0:T(8,128)(2,1)} %glog_hbm.1, f32[24,128]{1,0:T(8,128)} %master_hbm.1, f32[24,128]{1,0:T(8,128)} %one_hbm.1, f32[24,128]{1,0:T(8,128)} %two_hbm.1), custom_call_target="tpu_custom_call" | custom-call | flops 805306368 | bytes 3145728 | tf_op jit(solution)/shard_map/pallas_call | solution.py:358
  55.0 0.0 copy-done.2
  55.0 0.0 copy-done.1
  55.0 0.0 copy-done
  55.0 0.6 %multiply_subtract_fusion = (f32[24,128]{1,0:T(8,128)}, f32[24,128]{1,0:T(8,128)}, f32[24,128]{1,0:T(8,128)}) fusion(f32[24,128]{1,0:T(8,128)S(1)} %copy-done, f32[]{:T(128)} %bitcast.1, f32[]{:T(128)} %bitcast, f32[24,128]{1,0:T(8,128)S(1)} %get-tuple-element.6, f32[24,128]{1,0:T(8,128)S(1)} %copy-done.2, f32[24,128]{1,0:T(8,128)S(1)} %copy-done.1), kind=kLoop, calls=%fused_computation.2 | loop fusion | flops 46080 | bytes 86024 | tf_op jit(solution)/shard_map/sub | solution.py:403
  55.7 0.6 %copy.11 = bf16[256,128]{1,0:T(8,128)(2,1)} copy(bf16[256,128]{1,0:T(8,128)(2,1)S(1)} %get-tuple-element.14) | data formatting | bytes 131072
Async XLA Ops:
  0.6 54.4 %copy-start.2 = (f32[24,128]{1,0:T(8,128)S(1)}, f32[24,128]{1,0:T(8,128)}, u32[]{:S(2)}) copy-start(f32[24,128]{1,0:T(8,128)} %two_hbm.1) | copy-start | bytes 36868
  0.6 54.4 %copy-start.1 = (f32[24,128]{1,0:T(8,128)S(1)}, f32[24,128]{1,0:T(8,128)}, u32[]{:S(2)}) copy-start(f32[24,128]{1,0:T(8,128)} %one_hbm.1) | copy-start | bytes 36868
  0.7 54.4 %copy-start = (f32[24,128]{1,0:T(8,128)S(1)}, f32[24,128]{1,0:T(8,128)}, u32[]{:S(2)}) copy-start(f32[24,128]{1,0:T(8,128)} %master_hbm.1) | copy-start | bytes 36868

commit v5 on v4

--- a/solution.py
+++ b/solution.py
@@ -88,13 +88,13 @@
     barrier = pltpu.get_barrier_semaphore()
     for h, d, e in PARTNERS:
         pl.semaphore_signal(barrier, inc=1, device_id=at(h, d, 0, e), device_id_type=pl.DeviceIdType.MESH)
-    glog_load = load(glog_hbm, glog_ref, 16)
-    loads = []
+    glog_load = load(glog_hbm, glog_ref, 0)
     for k in range(4):
         cols = pl.ds(k * 1536, 1536)
-        loads.append(load(acts_hbm.at[:, cols], acts.at[:, cols], k))
-    loads_state = [load(ref, state.at[k], 17 + k) for k, ref in enumerate((master_hbm, one_hbm, two_hbm))]
-    loads_state.append(load(step_hbm, step_ref, 20))
+        load(acts_hbm.at[:, cols], acts.at[:, cols], 1)
+    for k, ref in enumerate((master_hbm, one_hbm, two_hbm)):
+        load(ref, state.at[k], 2)
+    step_load = load(step_hbm, step_ref, 3)
     mod = rep * 2 + core
     primary = lax.rem(z, 4) == mod
     rank = sum(jnp.where(z == place, k, 0) for k, place in enumerate(ORDER))
@@ -118,8 +118,13 @@
             device_id=device, device_id_type=pl.DeviceIdType.MESH,
         )
 
-    for copy in loads:
-        copy.wait()
+    def arrived(ref, sem):
+        remote(ref, ref, sem, sem, along_z(1)).wait_recv()
+
+    def left(ref, sem):
+        remote(ref, ref, sem, sem, along_z(1)).wait_send()
+
+    pltpu.make_async_copy(acts_hbm, acts, load_sem.at[1]).wait()
     for h, k in CHUNKS:
         q = h * 2 + k
         for px in range(4):
@@ -134,32 +139,24 @@
                     which, inner = (px, py) if h == 0 else (py, px)
                     part[q, which * 2 + pc, inner * UNIT:(inner + 1) * UNIT] = product[lo:lo + UNIT]
 
-    sent = []
-    copy_0 = {}
-    copy_a = {}
     pl.semaphore_wait(barrier, expected)
     for h, k in CHUNKS:
         q = h * 2 + k
         for d in STEPS:
             lane = lax.rem(main[h] + d, 4)
             copy = remote(
-                part.at[q, lane * 2 + 1 - core], pair.at[q, d], s0.at[q, d], r0.at[q, d], at(h, 0, 0, 1)
+                part.at[q, lane * 2 + 1 - core], pair.at[q, d], s0.at[0], r0.at[q], at(h, 0, 0, 1)
             )
             copy.start()
-            copy_0[h, k, d] = copy
-            sent.append(copy)
-    for h, k in CHUNKS:
-        q = h * 2 + k
-        for d in STEPS:
-            copy_0[h, k, d].wait_recv()
+    for h, k in CHUNKS:
+        q = h * 2 + k
+        arrived(pair.at[q], r0.at[q])
         for d in (2, 1, 3):
             total = part[q, lax.rem(main[h] + d, 4) * 2 + core].astype(F32) + pair[q, d].astype(F32)
             code[q, d, :ROWS], code[q, d, ROWS:] = encode(total)
         for d in (2, 1, 3):
-            copy = remote(code.at[q, d], recv_a.at[q, d], sa.at[q, d], ra.at[q, d], at(h, d, 0, 0))
-            copy.start()
-            copy_a[h, k, d] = copy
-            sent.append(copy)
+            copy = remote(code.at[q, d], recv_a.at[q, d], sa.at[0], ra.at[q], at(h, d, 0, 0))
+            copy.start()
     for k, place in enumerate(ORDER):
         @pl.when(jnp.logical_and(primary, rank > k))
         def _():
@@ -167,20 +164,17 @@
                 ready.at[z // 4], inc=1, device_id=dev(x, y, place, core), device_id_type=pl.DeviceIdType.MESH
             )
 
-    for copy in loads_state:
-        copy.wait()
+    step_load.wait()
+    pltpu.make_async_copy(state, state, load_sem.at[2]).wait()
     half = pl.ds(pl.multiple_of(core * OWN, 8), OWN)
     state48[:, half, :] = state[...]
     state_copy = remote(state, state48.at[:, half, :], st_sem.at[0], st_sem.at[1], at(0, 0, 0, 1))
     state_copy.start()
-    sent.append(state_copy)
-
-    copy_b = {}
+
     for h, k in CHUNKS:
         q = h * 2 + k
         mine = main[h] * 2 + core
-        for d in (1, 3, 2):
-            copy_a[h, k, d].wait_recv()
+        arrived(recv_a.at[q, 1:4], ra.at[q])
         units = {d: decode_unit(recv_a[q, d, ROWS:]) for d in (1, 3, 2)}
         for d in (2, 1, 3, 0):
             to = lax.rem(cross[h] + d, 4)
@@ -191,20 +185,17 @@
             acc[q, d] = total
         for d in (2, 1, 3, 0):
             if d:
-                copy = remote(acc.at[q, d], recv_b.at[q, d], sb.at[q, d], rb.at[q, d], at(h, 0, d, 0))
+                copy = remote(acc.at[q, d], recv_b.at[q, d], sb.at[0], rb.at[q], at(h, 0, d, 0))
                 copy.start()
-                copy_b[h, k, d] = copy
-                sent.append(copy)
 
     copy_c = []
     for h, k in CHUNKS:
         zg = h * 2 + k
-        for d in (1, 3, 2):
-            copy_b[h, k, d].wait_recv()
+        arrived(recv_b.at[zg, 1:4], rb.at[zg])
         unit[zg] = ((acc[zg, 0] + recv_b[zg, 1]) + recv_b[zg, 3]) + recv_b[zg, 2]
         to = zg * 4 + mod
         dz = lax.rem(to + 16 - z, 16)
-        copy = remote(unit.at[zg], recv_c.at[z], sc.at[zg], rc.at[z], dev(x, y, to, core))
+        copy = remote(unit.at[zg], recv_c.at[z], sc.at[zg], rc.at[0], dev(x, y, to, core))
         copy_c.append((copy, dz))
         rank_to = sum(jnp.where(to == place, j, 0) for j, place in enumerate(ORDER))
 
@@ -222,9 +213,10 @@
 
     scales = corrections(step_ref[0].astype(F32))
     state_copy.wait_recv()
-    for copy in sent:
-        copy.wait_send()
-    sent = []
+    state_copy.wait_send()
+    left(pair, s0.at[0])
+    left(code.at[0:3], sa.at[0])
+    left(acc.at[0:3], sb.at[0])
     other = pl.ds(pl.multiple_of((1 - core) * OWN, 8), OWN)
 
     def place(zg):
@@ -236,22 +228,20 @@
     zg_me = z // 4
     spot = place(zg_me)
     copy_z = {
-        to: remote(spot, spot, sz.at[to], rz.at[zg_me], dev(x, y, to, core)) for to in range(16)
+        to: remote(spot, spot, sz.at[0], rz.at[zg_me], dev(x, y, to, core)) for to in range(16)
     }
     copy_d = [
         remote(own48.at[half], grad_own, sd.at[0], rd.at[0], at(1, 2, 0, 0)),
-        remote(own48.at[other], grad_own, sd.at[1], rd.at[0], at(1, 0, 0, 1)),
-        remote(own48.at[other], grad_own, sd.at[2], rd.at[0], at(1, 2, 0, 1)),
+        remote(own48.at[other], grad_own, sd.at[0], rd.at[0], at(1, 0, 0, 1)),
+        remote(own48.at[other], grad_own, sd.at[0], rd.at[0], at(1, 2, 0, 1)),
     ]
 
     @pl.when(primary)
     def _():
         recv_c[z] = own48[...]
-        total = jnp.zeros((UNIT, E), F32)
-        for place in ORDER:
-            @pl.when(z != place)
-            def _():
-                remote(recv_c.at[place], recv_c.at[place], sc.at[0], rc.at[place], along_z(1)).wait_recv()
+        arrived(recv_c.at[0:15], rc.at[0])
+        total = recv_c[0]
+        for place in range(1, 16):
             total = total + recv_c[place]
         updated, _, _ = adam(total, state48[0], state48[1], state48[2], *scales)
         spot[...] = updated.astype(BF16)
@@ -264,7 +254,6 @@
             copy.start()
         grad_own[...] = own48[half]
 
-    copy_1 = {}
     for h, k in GATHER:
         zg = h * 2 + k
 
@@ -272,10 +261,8 @@
         def _():
             remote(place(zg), place(zg), sz.at[0], rz.at[zg], along_z(1)).wait_recv()
         for d in (2, 1, 3):
-            copy = remote(place(zg), place(zg), s1.at[zg, d], r1.at[zg, d], at(h, 0, d, 0))
-            copy.start()
-            copy_1[h, k, d] = copy
-            sent.append(copy)
+            copy = remote(place(zg), place(zg), s1.at[0], r1.at[zg], at(h, 0, d, 0))
+            copy.start()
 
     for copy, dz in copy_c:
         @pl.when(dz != 0)
@@ -283,26 +270,21 @@
             copy.wait_send()
 
     copy_2 = {}
-    copy_3 = {}
 
     def forward(h, k, d):
         q = h * 2 + k
         lane = wnew.at[q, lax.rem(main[h] + d, 4) * 2 + core]
-        copy = remote(lane, lane, s3.at[q, d], r3.at[q, d], at(h, 0, 0, 1))
+        copy = remote(lane, lane, s3.at[0], r3.at[q], at(h, 0, 0, 1))
         copy.start()
-        copy_3[h, k, d] = copy
-        sent.append(copy)
 
     for h, k in GATHER:
         q = h * 2 + k
-        for d in (1, 3, 2):
-            copy_1[h, k, d].wait_recv()
+        arrived(wnew.at[q, 0, 0:3 * UNIT], r1.at[q])
         mine = wnew.at[q, main[h] * 2 + core]
         for d in (2, 1, 3):
-            copy = remote(mine, mine, s2.at[q, d], r2.at[q, d], at(h, d, 0, 0))
+            copy = remote(mine, mine, s2.at[0], r2.at[q, d - 1], at(h, d, 0, 0))
             copy.start()
             copy_2[h, k, d] = copy
-            sent.append(copy)
         forward(h, k, 0)
 
     @pl.when(jnp.logical_not(primary))
@@ -313,19 +295,14 @@
 
     @pl.when(primary)
     def _():
-        for to in range(16):
-            @pl.when(z != to)
-            def _():
-                copy_z[to].wait_send()
-        for copy in copy_d:
-            copy.wait_send()
+        left(acts.at[0:240, 0:BLK], sz.at[0])
+        left(state, sd.at[0])
 
     logits = jnp.zeros((TOK, E), F32)
 
     def apply(total, h, k):
         q = h * 2 + k
-        for d in range(4):
-            copy_3[h, k, d].wait_recv()
+        arrived(wnew.at[q, 0:4], r3.at[q])
         for lane in range(4):
             weights = []
             for zr in range(4):
@@ -346,8 +323,9 @@
     logits = apply(logits, *GATHER[-1])
     logits_out[...] = logits.astype(BF16)
 
-    for copy in sent:
-        copy.wait_send()
+    left(wnew.at[0, 0:3], s1.at[0])
+    left(wnew.at[0:3, 0:4], s2.at[0])
+    left(wnew.at[0:2], s3.at[0])
 
 
 def per_device(acts, grad_logits, master, moment_one, moment_two, step_count):
@@ -379,16 +357,16 @@
             pltpu.VMEM((3, UNIT, E), F32),
             pltpu.VMEM((OWN, E), F32),
             pltpu.VMEM((4, 8, 4 * UNIT, E), BF16),
-            dma((21,)), dma((2,)), pltpu.SemaphoreType.REGULAR((4,)),
-            dma((4, 4)), dma((4, 4)),
-            dma((4, 4)), dma((4, 4)),
-            dma((4, 4)), dma((4, 4)),
-            dma((4,)), dma((16,)),
-            dma((3,)), dma((1,)),
-            dma((16,)), dma((4,)),
-            dma((4, 4)), dma((4, 4)),
-            dma((4, 4)), dma((4, 4)),
-            dma((4, 4)), dma((4, 4)),
+            dma((4,)), dma((2,)), pltpu.SemaphoreType.REGULAR((4,)),
+            dma((1,)), dma((4,)),
+            dma((1,)), dma((4,)),
+            dma((1,)), dma((4,)),
+            dma((4,)), dma((1,)),
+            dma((1,)), dma((1,)),
+            dma((1,)), dma((4,)),
+            dma((1,)), dma((4,)),
+            dma((1,)), dma((4, 3)),
+            dma((1,)), dma((4,)),
         ],
         compiler_params=pltpu.CompilerParams(
             collective_id=0, has_side_effects=True, vmem_limit_bytes=60 * 1024 * 1024

time: 56.5 us -> 54.4 us (0.963)
  Pallas kernels: 53.6 us -> 51.5 us
    pallas_call x1, Pallas kernels: 53.6 us -> 51.5 us  [per_device(): pl.pallas_call(kernel, out_shape=(pltpu.VMEM((OWN, E), F32), pltpu.VMEM((...]
where the time goes in v5:
time: 54.4 us; the launch traced here: 54.3 us
  Pallas kernels  51.5 us (95%)
  between operations  1.44 us (3%)
  local copies, waits for them, and re-layouts  0.64 us (1%)
  other arithmetic  0.64 us (1%)
    pallas_call x1, Pallas kernels, per_device(): pl.pallas_call(kernel, out_shape=(pltpu.VMEM((OWN, E), F32), pltpu.VMEM((...  51.5 us

profile of v5, /device:TPU:1, one launch (start us, length us, event | category | flops | bytes accessed | tf_op | source)
XLA Modules:
  0.0 54.3 jit_solution(15773907699594683628)
XLA Ops:
  0.6 0.0 copy-start.2
  0.6 0.0 copy-start.1
  0.7 0.0 copy-start
  1.4 51.5 %shard_map.93 = (f32[24,128]{1,0:T(8,128)S(1)}, bf16[256,128]{1,0:T(8,128)(2,1)S(1)}) custom-call(s32[1]{0:T(128)S(6)} %copy.12.step_hbm, bf16[256,6144]{1,0:T(8,128)(2,1)} %acts_hbm.1, bf16[256,128]{1,0:T(8,128)(2,1)} %glog_hbm.1, f32[24,128]{1,0:T(8,128)} %master_hbm.1, f32[24,128]{1,0:T(8,128)} %one_hbm.1, f32[24,128]{1,0:T(8,128)} %two_hbm.1), custom_call_target="tpu_custom_call" | custom-call | flops 805306368 | bytes 3145728 | tf_op jit(solution)/shard_map/pallas_call | solution.py:336
  53.0 0.0 copy-done.2
  53.0 0.0 copy-done.1
  53.0 0.0 copy-done
  53.0 0.6 %multiply_subtract_fusion = (f32[24,128]{1,0:T(8,128)}, f32[24,128]{1,0:T(8,128)}, f32[24,128]{1,0:T(8,128)}) fusion(f32[24,128]{1,0:T(8,128)S(1)} %copy-done, f32[]{:T(128)} %bitcast.1, f32[]{:T(128)} %bitcast, f32[24,128]{1,0:T(8,128)S(1)} %get-tuple-element.6, f32[24,128]{1,0:T(8,128)S(1)} %copy-done.2, f32[24,128]{1,0:T(8,128)S(1)} %copy-done.1), kind=kLoop, calls=%fused_computation.2 | loop fusion | flops 46080 | bytes 86024 | tf_op jit(solution)/shard_map/sub | solution.py:381
  53.6 0.6 %copy.11 = bf16[256,128]{1,0:T(8,128)(2,1)} copy(bf16[256,128]{1,0:T(8,128)(2,1)S(1)} %get-tuple-element.14) | data formatting | bytes 131072
Async XLA Ops:
  0.6 52.3 %copy-start.2 = (f32[24,128]{1,0:T(8,128)S(1)}, f32[24,128]{1,0:T(8,128)}, u32[]{:S(2)}) copy-start(f32[24,128]{1,0:T(8,128)} %two_hbm.1) | copy-start | bytes 36868
  0.6 52.3 %copy-start.1 = (f32[24,128]{1,0:T(8,128)S(1)}, f32[24,128]{1,0:T(8,128)}, u32[]{:S(2)}) copy-start(f32[24,128]{1,0:T(8,128)} %one_hbm.1) | copy-start | bytes 36868
  0.7 52.3 %copy-start = (f32[24,128]{1,0:T(8,128)S(1)}, f32[24,128]{1,0:T(8,128)}, u32[]{:S(2)}) copy-start(f32[24,128]{1,0:T(8,128)} %master_hbm.1) | copy-start | bytes 36868

commit v6 on v5

--- a/solution.py
+++ b/solution.py
@@ -110,7 +110,7 @@
         expected = expected + jnp.where(jnp.logical_and(meets, rank > k), 1, 0)
 
     glog_load.wait()
-    glog = glog_ref[...]
+    glog = glog_ref[...].T
 
     def remote(src, dst, send, recv, device):
         return pltpu.make_async_remote_copy(
@@ -129,9 +129,7 @@
         q = h * 2 + k
         for px in range(4):
             cols = pl.ds(px * 1536 + q * BLK, BLK)
-            product = lax.dot_general(
-                glog, acts[:, cols], (((0,), (0,)), ((), ())), preferred_element_type=F32
-            ).T.astype(BF16)
+            product = jnp.dot(glog, acts[:, cols], preferred_element_type=F32).T.astype(BF16)
             for zr in range(4):
                 for ylo in range(2):
                     lo = (zr * 2 + ylo) * UNIT
@@ -192,7 +190,8 @@
     for h, k in CHUNKS:
         zg = h * 2 + k
         arrived(recv_b.at[zg, 1:4], rb.at[zg])
-        unit[zg] = ((acc[zg, 0] + recv_b[zg, 1]) + recv_b[zg, 3]) + recv_b[zg, 2]
+        total = ((acc[zg, 0] + recv_b[zg, 1]) + recv_b[zg, 3]) + recv_b[zg, 2]
+        unit[zg, :UNIT], unit[zg, UNIT:] = encode(total)
         to = zg * 4 + mod
         dz = lax.rem(to + 16 - z, 16)
         copy = remote(unit.at[zg], recv_c.at[z], sc.at[zg], rc.at[0], dev(x, y, to, core))
@@ -209,7 +208,7 @@
 
         @pl.when(dz == 0)
         def _():
-            own48[...] = unit[zg]
+            own48[...] = total
 
     scales = corrections(step_ref[0].astype(F32))
     state_copy.wait_recv()
@@ -238,11 +237,11 @@
 
     @pl.when(primary)
     def _():
-        recv_c[z] = own48[...]
+        recv_c[z] = jnp.zeros((UNIT + 16, E), jnp.int16)
         arrived(recv_c.at[0:15], rc.at[0])
-        total = recv_c[0]
-        for place in range(1, 16):
-            total = total + recv_c[place]
+        total = own48[...]
+        for place in range(16):
+            total = total + recv_c[place, :UNIT].astype(jnp.int32).astype(F32) * decode_unit(recv_c[place, UNIT:])
         updated, _, _ = adam(total, state48[0], state48[1], state48[2], *scales)
         spot[...] = updated.astype(BF16)
         for to in (0, 1, 2, 3, 4, 15, 5, 14, 6, 13, 7, 12, 8, 11, 9, 10):
@@ -350,8 +349,8 @@
             pltpu.VMEM((4, 4, ROWS + 16, E), jnp.int16),
             pltpu.VMEM((4, 4, UNIT, E), F32),
             pltpu.VMEM((4, 4, UNIT, E), F32),
-            pltpu.VMEM((4, UNIT, E), F32),
-            pltpu.VMEM((16, UNIT, E), F32),
+            pltpu.VMEM((4, UNIT + 16, E), jnp.int16),
+            pltpu.VMEM((16, UNIT + 16, E), jnp.int16),
             pltpu.VMEM((UNIT, E), F32),
             pltpu.VMEM((3, OWN, E), F32),
             pltpu.VMEM((3, UNIT, E), F32),

time: 54.4 us -> 54.1 us (level)
  no operation moved by 1% of the time
where the time goes in v6:
time: 54.1 us; the launch traced here: 53.9 us
  Pallas kernels  51.2 us (95%)
  between operations  1.44 us (3%)
  local copies, waits for them, and re-layouts  0.64 us (1%)
  other arithmetic  0.64 us (1%)
    pallas_call x1, Pallas kernels, per_device(): pl.pallas_call(kernel, out_shape=(pltpu.VMEM((OWN, E), F32), pltpu.VMEM((...  51.2 us

profile of v6, /device:TPU:1, one launch (start us, length us, event | category | flops | bytes accessed | tf_op | source)
XLA Modules:
  0.0 53.9 jit_solution(15567150464212999627)
XLA Ops:
  0.6 0.0 copy-start.2
  0.6 0.0 copy-start.1
  0.7 0.0 copy-start
  1.4 51.2 %shard_map.93 = (f32[24,128]{1,0:T(8,128)S(1)}, bf16[256,128]{1,0:T(8,128)(2,1)S(1)}) custom-call(s32[1]{0:T(128)S(6)} %copy.12.step_hbm, bf16[256,6144]{1,0:T(8,128)(2,1)} %acts_hbm.1, bf16[256,128]{1,0:T(8,128)(2,1)} %glog_hbm.1, f32[24,128]{1,0:T(8,128)} %master_hbm.1, f32[24,128]{1,0:T(8,128)} %one_hbm.1, f32[24,128]{1,0:T(8,128)} %two_hbm.1), custom_call_target="tpu_custom_call" | custom-call | flops 805306368 | bytes 3145728 | tf_op jit(solution)/shard_map/pallas_call | solution.py:335
  52.6 0.0 copy-done.2
  52.6 0.0 copy-done.1
  52.7 0.0 copy-done
  52.7 0.6 %multiply_subtract_fusion = (f32[24,128]{1,0:T(8,128)}, f32[24,128]{1,0:T(8,128)}, f32[24,128]{1,0:T(8,128)}) fusion(f32[24,128]{1,0:T(8,128)S(1)} %copy-done, f32[]{:T(128)} %bitcast.1, f32[]{:T(128)} %bitcast, f32[24,128]{1,0:T(8,128)S(1)} %get-tuple-element.6, f32[24,128]{1,0:T(8,128)S(1)} %copy-done.2, f32[24,128]{1,0:T(8,128)S(1)} %copy-done.1), kind=kLoop, calls=%fused_computation.2 | loop fusion | flops 46080 | bytes 86024 | tf_op jit(solution)/shard_map/sub | solution.py:380
  53.3 0.6 %copy.11 = bf16[256,128]{1,0:T(8,128)(2,1)} copy(bf16[256,128]{1,0:T(8,128)(2,1)S(1)} %get-tuple-element.14) | data formatting | bytes 131072
Async XLA Ops:
  0.6 52.0 %copy-start.2 = (f32[24,128]{1,0:T(8,128)S(1)}, f32[24,128]{1,0:T(8,128)}, u32[]{:S(2)}) copy-start(f32[24,128]{1,0:T(8,128)} %two_hbm.1) | copy-start | bytes 36868
  0.6 52.0 %copy-start.1 = (f32[24,128]{1,0:T(8,128)S(1)}, f32[24,128]{1,0:T(8,128)}, u32[]{:S(2)}) copy-start(f32[24,128]{1,0:T(8,128)} %one_hbm.1) | copy-start | bytes 36868
  0.7 52.0 %copy-start = (f32[24,128]{1,0:T(8,128)S(1)}, f32[24,128]{1,0:T(8,128)}, u32[]{:S(2)}) copy-start(f32[24,128]{1,0:T(8,128)} %master_hbm.1) | copy-start | bytes 36868

commit v7 on v6

--- a/solution.py
+++ b/solution.py
@@ -58,7 +58,7 @@
 def kernel(
     step_hbm, acts_hbm, glog_hbm, master_hbm, one_hbm, two_hbm,
     grad_out, logits_out,
-    step_ref, acts, glog_ref, part, pair, code, recv_a, acc, recv_b, unit, recv_c, own48, state, state48, grad_own, wnew,
+    step_ref, acts, glog_ref, part, pair, code, recv_a, acc, held, recv_b, unit, recv_c, own48, state, state48, grad_own, wnew,
     load_sem, st_sem, ready, s0, r0, sa, ra, sb, rb, sc, rc, sd, rd, sz, rz, s1, r1, s2, r2, s3, r3,
 ):
     seq = lax.axis_index("seq")
@@ -180,17 +180,22 @@
             total = part[q, mine, rows].astype(F32) + pair[q, 0, rows].astype(F32)
             for p in (1, 3, 2):
                 total = total + recv_a[q, p, rows].astype(jnp.int32).astype(F32) * units[p]
-            acc[q, d] = total
+            if d:
+                acc[q, d - 1, :UNIT], acc[q, d - 1, UNIT:] = encode(total)
+            else:
+                held[q] = total
         for d in (2, 1, 3, 0):
             if d:
-                copy = remote(acc.at[q, d], recv_b.at[q, d], sb.at[0], rb.at[q], at(h, 0, d, 0))
+                copy = remote(acc.at[q, d - 1], recv_b.at[q, d - 1], sb.at[0], rb.at[q], at(h, 0, d, 0))
                 copy.start()
 
     copy_c = []
     for h, k in CHUNKS:
         zg = h * 2 + k
-        arrived(recv_b.at[zg, 1:4], rb.at[zg])
-        total = ((acc[zg, 0] + recv_b[zg, 1]) + recv_b[zg, 3]) + recv_b[zg, 2]
+        arrived(recv_b.at[zg], rb.at[zg])
+        total = held[zg]
+        for d in range(3):
+            total = total + recv_b[zg, d, :UNIT].astype(jnp.int32).astype(F32) * decode_unit(recv_b[zg, d, UNIT:])
         unit[zg, :UNIT], unit[zg, UNIT:] = encode(total)
         to = zg * 4 + mod
         dz = lax.rem(to + 16 - z, 16)
@@ -215,7 +220,7 @@
     state_copy.wait_send()
     left(pair, s0.at[0])
     left(code.at[0:3], sa.at[0])
-    left(acc.at[0:3], sb.at[0])
+    left(acc, sb.at[0])
     other = pl.ds(pl.multiple_of((1 - core) * OWN, 8), OWN)
 
     def place(zg):
@@ -347,8 +352,9 @@
             pltpu.VMEM((4, 4, ROWS, E), BF16),
             pltpu.VMEM((4, 4, ROWS + 16, E), jnp.int16),
             pltpu.VMEM((4, 4, ROWS + 16, E), jnp.int16),
-            pltpu.VMEM((4, 4, UNIT, E), F32),
-            pltpu.VMEM((4, 4, UNIT, E), F32),
+            pltpu.VMEM((4, 3, UNIT + 16, E), jnp.int16),
+            pltpu.VMEM((4, UNIT, E), F32),
+            pltpu.VMEM((4, 3, UNIT + 16, E), jnp.int16),
             pltpu.VMEM((4, UNIT + 16, E), jnp.int16),
             pltpu.VMEM((16, UNIT + 16, E), jnp.int16),
             pltpu.VMEM((UNIT, E), F32),

time: 54.1 us -> 54 us (level)
  no operation moved by 1% of the time
where the time goes in v7:
time: 54 us; the launch traced here: 53.8 us
  Pallas kernels  51.1 us (95%)
  between operations  1.44 us (3%)
  local copies, waits for them, and re-layouts  0.64 us (1%)
  other arithmetic  0.64 us (1%)
    pallas_call x1, Pallas kernels, per_device(): pl.pallas_call(kernel, out_shape=(pltpu.VMEM((OWN, E), F32), pltpu.VMEM((...  51.1 us

profile of v7, /device:TPU:1, one launch (start us, length us, event | category | flops | bytes accessed | tf_op | source)
XLA Modules:
  0.0 53.8 jit_solution(13644477890655154876)
XLA Ops:
  0.6 0.0 copy-start.2
  0.6 0.0 copy-start.1
  0.7 0.0 copy-start
  1.4 51.1 %shard_map.93 = (f32[24,128]{1,0:T(8,128)S(1)}, bf16[256,128]{1,0:T(8,128)(2,1)S(1)}) custom-call(s32[1]{0:T(128)S(6)} %copy.12.step_hbm, bf16[256,6144]{1,0:T(8,128)(2,1)} %acts_hbm.1, bf16[256,128]{1,0:T(8,128)(2,1)} %glog_hbm.1, f32[24,128]{1,0:T(8,128)} %master_hbm.1, f32[24,128]{1,0:T(8,128)} %one_hbm.1, f32[24,128]{1,0:T(8,128)} %two_hbm.1), custom_call_target="tpu_custom_call" | custom-call | flops 805306368 | bytes 3145728 | tf_op jit(solution)/shard_map/pallas_call | solution.py:340
  52.5 0.0 copy-done.2
  52.6 0.0 copy-done.1
  52.6 0.0 copy-done
  52.6 0.6 %multiply_subtract_fusion = (f32[24,128]{1,0:T(8,128)}, f32[24,128]{1,0:T(8,128)}, f32[24,128]{1,0:T(8,128)}) fusion(f32[24,128]{1,0:T(8,128)S(1)} %copy-done, f32[]{:T(128)} %bitcast.1, f32[]{:T(128)} %bitcast, f32[24,128]{1,0:T(8,128)S(1)} %get-tuple-element.6, f32[24,128]{1,0:T(8,128)S(1)} %copy-done.2, f32[24,128]{1,0:T(8,128)S(1)} %copy-done.1), kind=kLoop, calls=%fused_computation.2 | loop fusion | flops 46080 | bytes 86024 | tf_op jit(solution)/shard_map/sub | solution.py:386
  53.2 0.6 %copy.11 = bf16[256,128]{1,0:T(8,128)(2,1)} copy(bf16[256,128]{1,0:T(8,128)(2,1)S(1)} %get-tuple-element.14) | data formatting | bytes 131072
Async XLA Ops:
  0.6 51.9 %copy-start.2 = (f32[24,128]{1,0:T(8,128)S(1)}, f32[24,128]{1,0:T(8,128)}, u32[]{:S(2)}) copy-start(f32[24,128]{1,0:T(8,128)} %two_hbm.1) | copy-start | bytes 36868
  0.6 51.9 %copy-start.1 = (f32[24,128]{1,0:T(8,128)S(1)}, f32[24,128]{1,0:T(8,128)}, u32[]{:S(2)}) copy-start(f32[24,128]{1,0:T(8,128)} %one_hbm.1) | copy-start | bytes 36868
  0.7 51.9 %copy-start = (f32[24,128]{1,0:T(8,128)S(1)}, f32[24,128]{1,0:T(8,128)}, u32[]{:S(2)}) copy-start(f32[24,128]{1,0:T(8,128)} %master_hbm.1) | copy-start | bytes 36868
